TPU v7x, 256 devices: a whole 4x4x8 slice. The times are simulated.
256 devices in a mesh: wide: 32 (over z, y), narrow: 8 (over x, core).
Axes of the slice: x: 4, y: 4, z: 8, core: 2. Of those that a mesh axis runs over, the one named last changes fastest.
Arguments:
- multipoles: bfloat16 [49, 128, 32, 128], P(None, 'wide', 'narrow'), may hold values from -6 to 6
- translate_far: bfloat16 [7, 7, 7, 49, 49], replicated, may hold values from -0.0625 to 0.0625
- translate_up: bfloat16 [8, 49, 49], replicated, may hold values from -0.3125 to 0.3125
Outputs:
- locals_fine: float32 [49, 128, 32, 128], P(None, 'wide', 'narrow')
- parents: bfloat16 [49, 64, 16, 64], P(None, 'wide', 'narrow')
- locals_coarse: float32 [49, 64, 16, 64], P(None, 'wide', 'narrow')
All inputs are finite; a program needn't handle non-finite values.
Results may differ from a plain program's by a relative error of at most 0.001.
Values may be sent and summed in bfloat16 or wider, within the bound.
No kernel may reach another device: no remote copies, remote signals or barrier semaphores. Data moves between devices by JAX's collectives and lax.ppermute only.
A program may use at most 128 MiB of HBM per device.

v0:
```python
import jax
import jax.numpy as jnp
from jax import lax
from jax.experimental import pallas as pl
from jax.experimental.pallas import tpu as pltpu
from jax.sharding import PartitionSpec as P

F32 = jnp.float32
BF16 = jnp.bfloat16
NT = (((1,), (1,)), ((), ()))
COEF = 49
SLOT = 64
NY = 128
HY = 64
FINE = 4 * NY
ROWS = FINE + 3 * HY
SEG = NY + 8
SUMS = 4 * SEG + HY
VMEM = 100 * 2**20 // 2


def dot(a, b):
    return jnp.dot(a, b, preferred_element_type=F32)


def eye(n):
    rows = lax.broadcasted_iota(jnp.int32, (n, n), 0)
    cols = lax.broadcasted_iota(jnp.int32, (n, n), 1)
    return jnp.where(rows == cols, 1.0, 0.0).astype(BF16)


def tables_kernel(far_ref, up_ref, out_ref, pairs_ref, wide_ref):
    step = pl.program_id(0)
    near = jnp.abs(step - 3) <= 1
    out_ref[...] = jnp.zeros_like(out_ref)

    def at_dy(dy, carry):
        close = jnp.logical_and(near, jnp.abs(dy - 3) <= 1)
        keep = jnp.where(close, 0.0, 1.0)
        for dz in range(7):
            block = far_ref[0, dz, dy]
            if abs(dz - 3) <= 1:
                block = (block.astype(F32) * keep).astype(BF16)
            for sz in range(3):
                for cz in range(2):
                    to = 2 * sz + 1 + cz - dz
                    if 0 <= to <= 1:
                        out_ref[dy, sz, 0, pl.ds(SLOT * cz, COEF), pl.ds(SLOT * to, COEF)] = block
        return carry

    lax.fori_loop(0, 7, at_dy, 0)

    @pl.when(step == 0)
    def _():
        wide_ref[...] = up_ref[...].astype(F32)
        pairs_ref[...] = jnp.zeros_like(pairs_ref)
        for child in range(8):
            block = wide_ref[pl.ds(child, COEF, stride=8), :].astype(BF16)
            pairs_ref[pl.ds(SLOT * (child // 2), COEF), pl.ds(SLOT * (child % 2), COEF)] = block


def make_tables(far, up):
    return pl.pallas_call(
        tables_kernel,
        grid=(7,),
        in_specs=[
            pl.BlockSpec((1, 7, 7, COEF, COEF), lambda i: (i, 0, 0, 0, 0)),
            pl.BlockSpec((8 * COEF, COEF), lambda i: (0, 0)),
        ],
        out_specs=[
            pl.BlockSpec((7, 3, 1, 128, 128), lambda i: (0, 0, i, 0, 0)),
            pl.BlockSpec((256, 128), lambda i: (0, 0)),
        ],
        out_shape=[
            jax.ShapeDtypeStruct((7, 3, 7, 128, 128), BF16),
            jax.ShapeDtypeStruct((256, 128), BF16),
        ],
        scratch_shapes=[pltpu.VMEM((8 * COEF, COEF), F32)],
        compiler_params=pltpu.CompilerParams(vmem_limit_bytes=VMEM),
        cost_estimate=pl.CostEstimate(flops=0, bytes_accessed=10_000_000, transcendentals=0),
        name="tables",
    )(far, up)


def pack_kernel(where_ref, own_ref, a_ref, b_ref, pairs_ref, out_ref, in_ref, par_ref, bricks, halves, shuffled):
    odd, core = where_ref[0], where_ref[1]
    tail = jnp.zeros((3, 16 * (SLOT - COEF), NY), F32)
    bricks[:, pl.ds(16 * COEF, 16 * (SLOT - COEF)), :] = tail
    bricks[1, pl.ds(0, 16 * COEF), :] = own_ref[...].astype(F32)
    bricks[2 - 2 * odd, pl.ds(0, 16 * COEF), :] = a_ref[...].astype(F32)
    bricks[2 * odd, pl.ds(0, 16 * COEF), :] = b_ref[...].astype(F32)
    unit = eye(NY)
    pairs = pairs_ref[...]
    low = lax.broadcasted_iota(jnp.int32, (HY, 128), 1) < SLOT
    for xq in range(6):
        for q in range(2):
            zp = q + core - 2 * q * core
            cells = []
            for cx in range(2):
                for cz in range(2):
                    first = (2 * (xq % 2) + cx) * 4 + 2 * zp + cz
                    cells.append(bricks[xq // 2, pl.ds(first, SLOT, stride=16), :].astype(BF16))
            cells = jnp.concatenate(cells, axis=0)
            turned = lax.dot_general(unit, cells, NT, preferred_element_type=F32).astype(BF16)
            if 1 <= xq <= 4:
                (out_ref if q == 0 else in_ref)[pl.ds((xq - 1) * NY, NY), :] = turned
            halves[zp] = dot(turned, pairs)
        first = halves[0, pl.ds(0, HY, stride=2), :] + pltpu.roll(halves[0, pl.ds(1, HY, stride=2), :], SLOT, 1)
        second = pltpu.roll(halves[1, pl.ds(0, HY, stride=2), :], SLOT, 1) + halves[1, pl.ds(1, HY, stride=2), :]
        parent = jnp.where(low, first, second).astype(BF16)
        for ref in (out_ref, in_ref):
            ref[pl.ds(FINE + (xq // 2) * HY, HY), pl.ds(128 * (xq % 2), 128)] = parent
        if xq // 2 == 1:
            turned = lax.dot_general(unit, parent, NT, preferred_element_type=F32)
            for z in range(2):
                shuffled[pl.ds((xq - 2) * 2 + z, COEF, stride=4), :] = turned[z * SLOT : z * SLOT + COEF]
    par_ref[...] = shuffled[...].astype(BF16)


def pack(where, own, a, b, pairs):
    vmem = pl.BlockSpec(memory_space=pltpu.VMEM)
    return pl.pallas_call(
        pack_kernel,
        in_specs=[pl.BlockSpec(memory_space=pltpu.SMEM)] + [vmem] * 4,
        out_specs=[vmem] * 3,
        out_shape=[
            jax.ShapeDtypeStruct((ROWS, 256), BF16),
            jax.ShapeDtypeStruct((ROWS, 256), BF16),
            jax.ShapeDtypeStruct((4 * COEF, HY), BF16),
        ],
        scratch_shapes=[
            pltpu.VMEM((3, 16 * SLOT, NY), F32),
            pltpu.VMEM((2, NY, 128), F32),
            pltpu.VMEM((4 * COEF, HY), F32),
        ],
        compiler_params=pltpu.CompilerParams(vmem_limit_bytes=VMEM),
        name="pack",
    )(where, own, a, b, pairs)


def operator(tables, at):
    return jnp.concatenate(
        [tables[at][1:7].reshape(6 * 128, 128), tables[at][0:6].reshape(6 * 128, 128)], axis=1
    )


def slabs(ref):
    part = [ref[pl.ds(x * NY, NY), :] for x in range(4)]
    return jnp.concatenate([jnp.concatenate(part[x : x + 3], axis=1) for x in range(2)], axis=0)


def coarse_slab(ref):
    return jnp.concatenate([ref[pl.ds(FINE + x * HY, HY), :] for x in range(3)], axis=1)


def clear_gaps(spread):
    for seg in range(5):
        spread[:, pl.ds(seg * SEG, 8), :] = jnp.zeros((7, 8, 256), F32)
    spread[:, pl.ds(8 + 4 * SEG + HY, 8), :] = jnp.zeros((7, 8, 256), F32)


def shifted(spread, seg):
    rows = NY if seg < 4 else HY
    even = lax.broadcasted_iota(jnp.int32, (rows, 256), 0) % 2 == 0
    total = None
    for dy in range(7):
        moved = spread[dy, pl.ds(5 + seg * SEG + dy, rows), :]
        if dy == 0:
            moved = jnp.where(even, 0.0, moved)
        if dy == 6:
            moved = jnp.where(even, moved, 0.0)
        total = moved if total is None else total + moved
    return total


def put(spread, fine_out, fine_in, coarse):
    for px in range(2):
        spread[pl.ds(8 + px * SEG, NY), :] = fine_out[px * NY : (px + 1) * NY]
        spread[pl.ds(8 + (2 + px) * SEG, NY), :] = fine_in[px * NY : (px + 1) * NY]
    spread[pl.ds(8 + 4 * SEG, HY), :] = coarse


def inner_kernel(where_ref, out_ref, in_ref, tables_ref, sums_ref, tables, spread, sems):
    sign = 1 - 2 * where_ref[1]

    def fetch(dy):
        return pltpu.make_async_copy(tables_ref.at[dy], tables.at[dy], sems.at[dy])

    for dy in range(7):
        fetch(dy).start()
    clear_gaps(spread)

    def at_dy(dy, carry):
        fetch(dy).wait()
        here = tables.at[dy]
        of_out, of_in = slabs(out_ref), slabs(in_ref)
        same = dot(jnp.concatenate([of_out, of_in, coarse_slab(out_ref)], axis=0), operator(here, 1))
        to_out = same[0:256] + dot(of_in, operator(here, 1 + sign))
        to_in = same[256:512] + dot(of_out, operator(here, 1 - sign))
        put(spread.at[dy], to_out, to_in, same[512:])
        return carry

    lax.fori_loop(0, 7, at_dy, 0)
    for seg in range(5):
        rows = NY if seg < 4 else HY
        sums_ref[pl.ds(seg * NY, rows), :] = shifted(spread, seg)


def inner(where, out, into, tables):
    vmem = pl.BlockSpec(memory_space=pltpu.VMEM)
    return pl.pallas_call(
        inner_kernel,
        in_specs=[pl.BlockSpec(memory_space=pltpu.SMEM), vmem, vmem, pl.BlockSpec(memory_space=pl.ANY)],
        out_specs=vmem,
        out_shape=jax.ShapeDtypeStruct((FINE + HY, 256), F32),
        scratch_shapes=[
            pltpu.VMEM((7, 3, 7, 128, 128), BF16),
            pltpu.VMEM((7, SUMS + 16, 256), F32),
            pltpu.SemaphoreType.DMA((7,)),
        ],
        compiler_params=pltpu.CompilerParams(vmem_limit_bytes=VMEM),
        cost_estimate=pl.CostEstimate(flops=3_000_000_000, bytes_accessed=6_000_000, transcendentals=0),
        name="inner",
    )(where, out, into, tables)


def outer_kernel(where_ref, cross_ref, pair_ref, tables_ref, inner_ref, fine_ref, coarse_ref, tables, spread, sems):
    core = where_ref[1]

    def fetch(dy, side):
        return pltpu.make_async_copy(tables_ref.at[dy, 2 * side], tables.at[dy, side], sems.at[dy, side])

    for dy in range(7):
        for side in range(2):
            fetch(dy, side).start()
    clear_gaps(spread)
    partner = pair_ref.at[1 - core]

    def at_dy(dy, carry):
        for side in range(2):
            fetch(dy, side).wait()
        here = tables.at[dy]
        by_cross = dot(jnp.concatenate([slabs(cross_ref), coarse_slab(cross_ref)], axis=0), operator(here, core))
        by_pair = dot(jnp.concatenate([slabs(partner), coarse_slab(partner)], axis=0), operator(here, 1 - core))
        put(spread.at[dy], by_cross[0:256], by_pair[0:256], by_cross[256:] + by_pair[256:])
        return carry

    lax.fori_loop(0, 7, at_dy, 0)
    for q in range(2):
        pz = q + core - 2 * q * core
        for px in range(2):
            seg = 2 * q + px
            done = (inner_ref[pl.ds(seg * NY, NY), :] + shifted(spread, seg)).T
            for child in range(4):
                first = (2 * px + child // 2) * 4 + 2 * pz + child % 2
                fine_ref[pl.ds(first, COEF, stride=16), :] = done[child * SLOT : child * SLOT + COEF]
    done = (inner_ref[pl.ds(FINE, HY), :] + shifted(spread, 4)).T
    for child in range(4):
        coarse_ref[pl.ds(child, COEF, stride=4), :] = done[child * SLOT : child * SLOT + COEF]


def outer(where, cross, pair, tables, sums):
    vmem = pl.BlockSpec(memory_space=pltpu.VMEM)
    return pl.pallas_call(
        outer_kernel,
        in_specs=[pl.BlockSpec(memory_space=pltpu.SMEM), vmem, vmem, pl.BlockSpec(memory_space=pl.ANY), vmem],
        out_specs=[vmem, vmem],
        out_shape=[
            jax.ShapeDtypeStruct((16 * COEF, NY), F32),
            jax.ShapeDtypeStruct((4 * COEF, HY), F32),
        ],
        scratch_shapes=[
            pltpu.VMEM((7, 2, 7, 128, 128), BF16),
            pltpu.VMEM((7, SUMS + 16, 256), F32),
            pltpu.SemaphoreType.DMA((7, 2)),
        ],
        compiler_params=pltpu.CompilerParams(vmem_limit_bytes=VMEM),
        cost_estimate=pl.CostEstimate(flops=2_000_000_000, bytes_accessed=5_000_000, transcendentals=0),
        name="outer",
    )(where, cross, pair, tables, sums)


def exchange(array, axis, start):
    count = lax.axis_size(axis)
    there = [(i, i + 1) for i in range(start, count - 1, 2)]
    return lax.ppermute(array, axis, there + [(j, i) for i, j in there])


def shards(multipoles, translate_far, translate_up):
    where = jnp.stack([lax.axis_index("wide") % 2, lax.axis_index("narrow") % 2]).astype(jnp.int32)
    a = exchange(multipoles, "wide", 0)
    b = exchange(multipoles, "wide", 1)
    tables, pairs = make_tables(translate_far, translate_up.transpose(1, 0, 2).reshape(8 * COEF, COEF))
    flat = lambda brick: brick.reshape(16 * COEF, NY)
    out, into, parents = pack(where, flat(multipoles), flat(a), flat(b), pairs)
    cross = exchange(out, "narrow", 1)
    count = lax.axis_size("narrow")
    pair = lax.all_gather(into, "narrow", axis_index_groups=[[i, i + 1] for i in range(0, count, 2)])
    sums = inner(where, out, into, tables)
    fine, coarse = outer(where, cross, pair, tables, sums)
    return (
        fine.reshape(COEF, 4, 4, NY),
        parents.reshape(COEF, 2, 2, HY),
        coarse.reshape(COEF, 2, 2, HY),
    )


def solution(mesh):
    return jax.shard_map(
        shards,
        mesh=mesh,
        in_specs=(P(None, "wide", "narrow", None), P(), P()),
        out_specs=(
            P(None, "wide", "narrow", None),
            P(None, "wide", "narrow", None),
            P(None, "wide", "narrow", None),
        ),
        check_vma=False,
    )
```

profile of v0, /device:TPU:113, one launch (start us, length us, event | category | flops | bytes accessed | tf_op | source)
XLA Modules:
  0.0 39.4 jit_solution(6367911636226337311)
XLA Ops:
  0.6 0.0 copy-start
  0.6 2.2 %collective-permute-start.1 = (bf16[49,4,4,128]{3,2,1,0:T(4,128)(2,1)}, bf16[49,4,4,128]{3,2,1,0:T(4,128)(2,1)S(1)}, u32[]{:S(2)}, u32[]{:S(2)}) collective-permute-start(bf16[49,4,4,128]{3,2,1,0:T(4,128)(2,1)} %param.3), channel_id=1, source_target_pairs={{8,16},{24,32},{40,48},{56,64},{72,80},{88,96},{104,112},{120,128}... | collective-permute-start | bytes 602120 | tf_op jit(solution)/shard_map/ppermute | solution.py:286
  2.9 3.4 %collective-permute-start = (bf16[49,4,4,128]{3,2,1,0:T(4,128)(2,1)}, bf16[49,4,4,128]{3,2,1,0:T(4,128)(2,1)S(1)}, u32[]{:S(2)}, u32[]{:S(2)}) collective-permute-start(bf16[49,4,4,128]{3,2,1,0:T(4,128)(2,1)} %param.3), channel_id=1, source_target_pairs={{0,8},{16,24},{32,40},{48,56},{64,72},{80,88},{96,104},{112,120},{... | collective-permute-start | bytes 602120 | tf_op jit(solution)/shard_map/ppermute | solution.py:286
  6.3 0.0 copy-start.1
  6.3 0.9 %copy-done.1 = bf16[8,49,49]{2,0,1:T(8,128)(2,1)S(1)} copy-done((bf16[8,49,49]{2,0,1:T(8,128)(2,1)S(1)}, bf16[8,49,49]{2,0,1:T(8,128)(2,1)}, u32[]{:S(2)}) %copy-start.1) | copy-done | bytes 38440
  7.2 9.8 %tables.1 = (bf16[7,3,7,128,128]{4,3,2,1,0:T(8,128)(2,1)}, bf16[256,128]{1,0:T(8,128)(2,1)S(1)}) custom-call(bf16[7,7,7,49,49]{4,3,2,1,0:T(8,128)(2,1)} %far_ref.1, bf16[392,49]{1,0:T(8,128)(2,1)S(1)} %bitcast.14), custom_call_target="tpu_custom_call" | custom-call | bytes 10000000 | tf_op jit(solution)/shard_map/tables/pallas_call | solution.py:63
  17.0 0.1 pad_add_fusion.where_ref
  17.1 0.0 collective-permute-done.1
  17.1 0.0 collective-permute-done
  17.1 0.0 copy-done
  17.1 2.0 %pack.1 = (bf16[704,256]{1,0:T(8,128)(2,1)S(1)}, bf16[704,256]{1,0:T(8,128)(2,1)S(1)}, bf16[196,64]{1,0:T(8,128)(2,1)S(1)}) custom-call(s32[2]{0:T(128)S(1)} %pad_add_fusion.where_ref, bf16[784,128]{1,0:T(8,128)(2,1)S(1)} %bitcast.11, bf16[784,128]{1,0:T(8,128)(2,1)S(1)} %bitcast.13, bf16[784,128]{1,0:T(8,128)(2,1)S(1)} %bitcast.12, ...), custom_call_target="tpu_custom_call" | custom-call | tf_op jit(solution)/shard_map/pack/pallas_call | solution.py:122
  19.1 4.2 %collective-permute-start.2 = (bf16[704,256]{1,0:T(8,128)(2,1)S(1)}, bf16[704,256]{1,0:T(8,128)(2,1)S(1)}, u32[]{:S(2)}, u32[]{:S(2)}) collective-permute-start(bf16[704,256]{1,0:T(8,128)(2,1)S(1)} %get-tuple-element.11.out_ref), channel_id=1, source_target_pairs={{1,2},{3,4},{5,6},{2,1},{4,3},{6,5},{9,10},{11,12},{13,14},{10,9},... | collective-permute-start | bytes 1081352 | tf_op jit(solution)/shard_map/ppermute | solution.py:286
  23.4 2.3 %all-gather = bf16[1408,256]{1,0:T(8,128)(2,1)S(1)} all-gather(bf16[704,256]{1,0:T(8,128)(2,1)S(1)} %get-tuple-element.12.in_ref), channel_id=2, replica_groups={{0,1},{2,3},{4,5},{6,7},{8,9},{10,11},{12,13},{14,15},{16,17},{18,19},{..., dimensions={0}, use_global_device_ids=true | all-gather | bytes 1081344 | tf_op jit(solution)/shard_map/all_gather | solution.py:298
  25.7 0.7 %reshape.32 = bf16[49,2,2,64]{3,2,1,0:T(2,128)(2,1)} reshape(bf16[196,64]{1,0:T(8,128)(2,1)S(1)} %get-tuple-element.15) | data formatting | bytes 50176 | tf_op jit(solution)/shard_map/reshape | solution.py:303
  26.4 6.4 %inner.1.inner_ref = f32[576,256]{1,0:T(8,128)S(1)} custom-call(s32[2]{0:T(128)S(1)} %pad_add_fusion.where_ref, bf16[704,256]{1,0:T(8,128)(2,1)S(1)} %get-tuple-element.11.out_ref, bf16[704,256]{1,0:T(8,128)(2,1)S(1)} %get-tuple-element.12.in_ref, bf16[7,3,7,128,128]{4,3,2,1,0:T(8,128)(2,1)} %get-tuple-element.13.tables_ref), custom_call_target="tpu_custom_call" | custom-call | flops 3000000000 | bytes 6000000 | tf_op jit(solution)/shard_map/inner/pallas_call | solution.py:211
  32.8 0.0 collective-permute-done.2.cross_ref
  32.8 5.9 %outer.1 = (f32[784,128]{1,0:T(8,128)}, f32[196,64]{1,0:T(8,128)S(1)}) custom-call(s32[2]{0:T(128)S(1)} %pad_add_fusion.where_ref, bf16[704,256]{1,0:T(8,128)(2,1)S(1)} %collective-permute-done.2.cross_ref, bf16[2,704,256]{2,1,0:T(8,128)(2,1)S(1)} %bitcast.10, bf16[7,3,7,128,128]{4,3,2,1,0:T(8,128)(2,1)} %get-tuple-element.13.tables_ref, ...), custom_call_target="tpu_custom_call" | custom-call | flops 2000000000 | bytes 5000000 | tf_op jit(solution)/shard_map/outer/pallas_call | solution.py:264
  38.7 0.7 %reshape.33 = f32[49,2,2,64]{3,2,1,0:T(2,128)} reshape(f32[196,64]{1,0:T(8,128)S(1)} %get-tuple-element.16) | data formatting | bytes 100352 | tf_op jit(solution)/shard_map/reshape | solution.py:304
Async XLA Ops:
  0.6 16.5 %copy-start = (bf16[49,4,4,128]{3,2,1,0:T(4,128)(2,1)S(1)}, bf16[49,4,4,128]{3,2,1,0:T(4,128)(2,1)}, u32[]{:S(2)}) copy-start(bf16[49,4,4,128]{3,2,1,0:T(4,128)(2,1)} %param.3) | copy-start | bytes 602116
  0.6 16.5 %collective-permute-start.1 = (bf16[49,4,4,128]{3,2,1,0:T(4,128)(2,1)}, bf16[49,4,4,128]{3,2,1,0:T(4,128)(2,1)S(1)}, u32[]{:S(2)}, u32[]{:S(2)}) collective-permute-start(bf16[49,4,4,128]{3,2,1,0:T(4,128)(2,1)} %param.3), channel_id=1, source_target_pairs={{8,16},{24,32},{40,48},{56,64},{72,80},{88,96},{104,112},{120,128}... | collective-permute-start | bytes 602120 | tf_op jit(solution)/shard_map/ppermute | solution.py:286
  2.9 14.2 %collective-permute-start = (bf16[49,4,4,128]{3,2,1,0:T(4,128)(2,1)}, bf16[49,4,4,128]{3,2,1,0:T(4,128)(2,1)S(1)}, u32[]{:S(2)}, u32[]{:S(2)}) collective-permute-start(bf16[49,4,4,128]{3,2,1,0:T(4,128)(2,1)} %param.3), channel_id=1, source_target_pairs={{0,8},{16,24},{32,40},{48,56},{64,72},{80,88},{96,104},{112,120},{... | collective-permute-start | bytes 602120 | tf_op jit(solution)/shard_map/ppermute | solution.py:286
  6.3 0.9 %copy-start.1 = (bf16[8,49,49]{2,0,1:T(8,128)(2,1)S(1)}, bf16[8,49,49]{2,0,1:T(8,128)(2,1)}, u32[]{:S(2)}) copy-start(bf16[8,49,49]{2,0,1:T(8,128)(2,1)} %param.5) | copy-start | bytes 115252
  19.1 13.7 %collective-permute-start.2 = (bf16[704,256]{1,0:T(8,128)(2,1)S(1)}, bf16[704,256]{1,0:T(8,128)(2,1)S(1)}, u32[]{:S(2)}, u32[]{:S(2)}) collective-permute-start(bf16[704,256]{1,0:T(8,128)(2,1)S(1)} %get-tuple-element.11.out_ref), channel_id=1, source_target_pairs={{1,2},{3,4},{5,6},{2,1},{4,3},{6,5},{9,10},{11,12},{13,14},{10,9},... | collective-permute-start | bytes 1081352 | tf_op jit(solution)/shard_map/ppermute | solution.py:286
where the time goes:
time: 39.8 us; the launch traced here: 39.4 us
  Pallas kernels  24.2 us (61%)
  starting transfers between devices  9.87 us (25%)
  blocking collectives  2.32 us (6%)
  local copies, waits for them, and re-layouts  2.28 us (6%)
  between operations  0.69 us (2%)
    ppermute x3, starting transfers between devices, exchange(): return lax.ppermute(array, axis, there + [(j, i) for i, j in there])  9.87 us
    pallas_call x1, Pallas kernels, make_tables(): pl.pallas_call(tables_kernel, grid=(7,), in_specs=[pl.BlockSpec((1, 7, 7,...  9.84 us
    pallas_call x1, Pallas kernels, inner(): pl.pallas_call(inner_kernel, in_specs=[pl.BlockSpec(memory_space=pltpu.SM...  6.4 us
    pallas_call x1, Pallas kernels, outer(): pl.pallas_call(outer_kernel, in_specs=[pl.BlockSpec(memory_space=pltpu.SM...  5.93 us
    all_gather x1, blocking collectives, shards(): lax.all_gather(into, 'narrow', axis_index_groups=[[i, i + 1] for i in ran...  2.32 us
    pallas_call x1, Pallas kernels, pack(): pl.pallas_call(pack_kernel, in_specs=[pl.BlockSpec(memory_space=pltpu.SME...  2.01 us
    unnamed x4, local copies, waits for them, and re-layouts  0.9 us
  transfers between devices with their start and end apart: 3, of which 0 were waited for; matrix products, arithmetic and copies ran while one was open for 2% of the time, Pallas kernels for 41%

commit v1 on v0

v1 whole, which is shorter than its diff:
```python
import jax
import jax.numpy as jnp
from jax import lax
from jax.experimental import pallas as pl
from jax.experimental.pallas import tpu as pltpu
from jax.sharding import PartitionSpec as P

F32 = jnp.float32
BF16 = jnp.bfloat16
NT = (((1,), (1,)), ((), ()))
COEF = 49
SLOT = 64
NY = 128
HY = 64
FINE = 4 * NY
ROWS = FINE + 3 * HY
SEG = NY + 8
SUMS = 4 * SEG + HY
VMEM = 20 * 2**20


def dot(a, b):
    return jnp.dot(a, b, preferred_element_type=F32)


def eye(n):
    rows = lax.broadcasted_iota(jnp.int32, (n, n), 0)
    cols = lax.broadcasted_iota(jnp.int32, (n, n), 1)
    return jnp.where(rows == cols, 1.0, 0.0).astype(BF16)


def core_parity():
    return lax.rem(lax.axis_index("narrow"), 2)


def turn(unit, bricks, brick, pair, zp):
    cells = []
    for cx in range(2):
        for cz in range(2):
            first = (2 * pair + cx) * 4 + 2 * zp + cz
            cells.append(bricks[brick, pl.ds(first, SLOT, stride=16), :].astype(BF16))
    cells = jnp.concatenate(cells, axis=0)
    return lax.dot_general(unit, cells, NT, preferred_element_type=F32).astype(BF16)


def to_parents(halves, at, low):
    z0, z1 = halves.at[at], halves.at[at + 1]
    first = z0[pl.ds(0, HY, stride=2), :] + pltpu.roll(z0[pl.ds(1, HY, stride=2), :], SLOT, 1)
    second = pltpu.roll(z1[pl.ds(0, HY, stride=2), :], SLOT, 1) + z1[pl.ds(1, HY, stride=2), :]
    return jnp.where(low, first, second).astype(BF16)


def lower_lanes():
    return lax.broadcasted_iota(jnp.int32, (HY, 128), 1) < SLOT


def early_kernel(
    far_hbm, own_hbm, up_hbm, tables_ref, slabs_ref, coarse_ref, pairs_ref, par_ref,
    far, own, up, bricks, wide, halves, shuffled, far_sems, sems,
):
    def fetch(dx):
        return pltpu.make_async_copy(far_hbm.at[dx], far.at[dx], far_sems.at[dx])

    get_own = pltpu.make_async_copy(own_hbm, own, sems.at[0])
    get_up = pltpu.make_async_copy(up_hbm, up, sems.at[1])
    get_own.start()
    get_up.start()
    for dx in range(7):
        fetch(dx).start()

    get_up.wait()
    wide[...] = up[...].astype(F32)
    pairs_ref[...] = jnp.zeros_like(pairs_ref)
    for child in range(8):
        block = wide[pl.ds(child, COEF, stride=8), :].astype(BF16)
        pairs_ref[pl.ds(SLOT * (child // 2), COEF), pl.ds(SLOT * (child % 2), COEF)] = block
    get_own.wait()
    bricks[0, pl.ds(16 * COEF, 16 * (SLOT - COEF)), :] = jnp.zeros((16 * (SLOT - COEF), NY), F32)
    bricks[0, pl.ds(0, 16 * COEF), :] = own[...].astype(F32)
    unit, low = eye(NY), lower_lanes()
    core = core_parity()
    for px in range(2):
        for q in range(2):
            zp = q + core - 2 * q * core
            turned = turn(unit, bricks, 0, px, zp)
            slabs_ref[pl.ds((2 * q + px) * NY, NY), :] = turned
            halves[2 * px + zp] = dot(turned, pairs_ref[...])
    for px in range(2):
        parent = to_parents(halves, 2 * px, low)
        coarse_ref[:, pl.ds(128 * px, 128)] = parent
        turned = lax.dot_general(unit, parent, NT, preferred_element_type=F32)
        for z in range(2):
            shuffled[pl.ds(2 * px + z, COEF, stride=4), :] = turned[z * SLOT : z * SLOT + COEF]
    par_ref[...] = shuffled[...].astype(BF16).reshape(COEF, 2, 2, HY)

    def at_dx(dx, carry):
        fetch(dx).wait()
        keep = jnp.where(jnp.abs(dx - 3) <= 1, 0.0, 1.0).astype(BF16)
        for dy in range(7):
            left, right = [], []
            for dz in range(7):
                block = far[dx, dz, dy]
                if abs(dz - 3) <= 1 and abs(dy - 3) <= 1:
                    block = block * keep
                block = jnp.pad(block, ((0, SLOT - COEF), (0, 128 - COEF)))
                left.append(block)
                right.append(jnp.concatenate([block[:, SLOT:], block[:, :SLOT]], axis=1))
            for sz in range(3):
                for cz in range(2):
                    tables_ref[dy, sz, dx, pl.ds(SLOT * cz, SLOT), :] = left[2 * sz + 1 + cz] + right[2 * sz + cz]
        return carry

    lax.fori_loop(0, 7, at_dx, 0)


def early(far, own, up):
    hbm = pl.BlockSpec(memory_space=pltpu.HBM)
    vmem = pl.BlockSpec(memory_space=pltpu.VMEM)
    return pl.pallas_call(
        early_kernel,
        in_specs=[hbm] * 3,
        out_specs=[vmem] * 5,
        out_shape=[
            pltpu.VMEM((7, 3, 7, 128, 128), BF16),
            pltpu.VMEM((FINE, 256), BF16),
            pltpu.VMEM((HY, 256), BF16),
            pltpu.VMEM((256, 128), BF16),
            jax.ShapeDtypeStruct((COEF, 2, 2, HY), BF16),
        ],
        scratch_shapes=[
            pltpu.VMEM((7, 7, 7, COEF, COEF), BF16),
            pltpu.VMEM((16 * COEF, NY), BF16),
            pltpu.VMEM((8 * COEF, COEF), BF16),
            pltpu.VMEM((1, 16 * SLOT, NY), F32),
            pltpu.VMEM((8 * COEF, COEF), F32),
            pltpu.VMEM((4, NY, 128), F32),
            pltpu.VMEM((4 * COEF, HY), F32),
            pltpu.SemaphoreType.DMA((7,)),
            pltpu.SemaphoreType.DMA((2,)),
        ],
        compiler_params=pltpu.CompilerParams(vmem_limit_bytes=VMEM),
        cost_estimate=pl.CostEstimate(flops=0, bytes_accessed=10_000_000, transcendentals=0),
        name="early",
    )(*[pltpu.with_memory_space_constraint(x, pltpu.HBM) for x in (far, own, up)])


def pack_kernel(a_ref, b_ref, slabs_ref, coarse_ref, pairs_ref, out_ref, in_ref, bricks, halves):
    odd, core = lax.rem(lax.axis_index("wide"), 2), core_parity()
    bricks[:, pl.ds(16 * COEF, 16 * (SLOT - COEF)), :] = jnp.zeros((2, 16 * (SLOT - COEF), NY), F32)
    bricks[1 - odd, pl.ds(0, 16 * COEF), :] = a_ref[...].astype(F32)
    bricks[odd, pl.ds(0, 16 * COEF), :] = b_ref[...].astype(F32)
    unit, low = eye(NY), lower_lanes()
    refs = (out_ref, in_ref)
    for q in range(2):
        refs[q][pl.ds(NY, 2 * NY), :] = slabs_ref[pl.ds(q * 2 * NY, 2 * NY), :]
        refs[q][pl.ds(FINE + HY, HY), :] = coarse_ref[...]
    for brick in range(2):
        for px in range(2):
            for q in range(2):
                zp = q + core - 2 * q * core
                turned = turn(unit, bricks, brick, px, zp)
                if px == 1 - brick:
                    refs[q][pl.ds(brick * 3 * NY, NY), :] = turned
                halves[4 * brick + 2 * px + zp] = dot(turned, pairs_ref[...])
    for brick in range(2):
        for px in range(2):
            parent = to_parents(halves, 4 * brick + 2 * px, low)
            for ref in refs:
                ref[pl.ds(FINE + 2 * brick * HY, HY), pl.ds(128 * px, 128)] = parent


def pack(a, b, own):
    vmem = pl.BlockSpec(memory_space=pltpu.VMEM)
    return pl.pallas_call(
        pack_kernel,
        in_specs=[vmem] * 5,
        out_specs=[vmem] * 2,
        out_shape=[jax.ShapeDtypeStruct((ROWS, 256), BF16)] * 2,
        scratch_shapes=[
            pltpu.VMEM((2, 16 * SLOT, NY), F32),
            pltpu.VMEM((8, NY, 128), F32),
        ],
        compiler_params=pltpu.CompilerParams(vmem_limit_bytes=VMEM),
        name="pack",
    )(a, b, *[pltpu.with_memory_space_constraint(x, pltpu.VMEM) for x in own])


def operator(tables, dy, at, skip=False):
    blocks = [tables[dy, at, dx] for dx in range(7)]
    return jnp.concatenate(
        [jnp.concatenate([blocks[e + 1], blocks[e]], axis=1) for e in range(6) if not (skip and e in (2, 3))],
        axis=0,
    )


def slabs(ref):
    part = [ref[pl.ds(x * NY, NY), :] for x in range(4)]
    return jnp.concatenate([jnp.concatenate(part[x : x + 3], axis=1) for x in range(2)], axis=0)


def coarse_slab(ref):
    return jnp.concatenate([ref[pl.ds(FINE + x * HY, HY), :] for x in range(3)], axis=1)


def clear_gaps(spread):
    for seg in range(5):
        spread[:, pl.ds(seg * SEG, 8), :] = jnp.zeros((7, 8, 256), F32)
    spread[:, pl.ds(8 + 4 * SEG + HY, 8), :] = jnp.zeros((7, 8, 256), F32)


def shifted(spread, seg):
    rows = NY if seg < 4 else HY
    even = lax.broadcasted_iota(jnp.int32, (rows, 256), 0) % 2 == 0
    total = None
    for dy in range(7):
        moved = spread[dy, pl.ds(5 + seg * SEG + dy, rows), :]
        if dy == 0:
            moved = jnp.where(even, 0.0, moved)
        if dy == 6:
            moved = jnp.where(even, moved, 0.0)
        total = moved if total is None else total + moved
    return total


def put(spread, fine_out, fine_in, coarse):
    for px in range(2):
        spread[pl.ds(8 + px * SEG, NY), :] = fine_out[px * NY : (px + 1) * NY]
        spread[pl.ds(8 + (2 + px) * SEG, NY), :] = fine_in[px * NY : (px + 1) * NY]
    spread[pl.ds(8 + 4 * SEG, HY), :] = coarse


def inner_kernel(out_ref, in_ref, tables, sums_ref, sources, spread):
    sign = 1 - 2 * core_parity()
    clear_gaps(spread)
    sources[...] = jnp.concatenate([slabs(out_ref), slabs(in_ref), coarse_slab(out_ref)], axis=0)
    for dy in range(7):
        if 2 <= dy <= 4:
            beside = jnp.concatenate([sources[:, 0:256], sources[:, 512:768]], axis=1)
            same = dot(beside, operator(tables, dy, 1, True))
        else:
            same = dot(sources[...], operator(tables, dy, 1))
        to_out = same[0:256] + dot(sources[256:512, :], operator(tables, dy, 1 + sign))
        to_in = same[256:512] + dot(sources[0:256, :], operator(tables, dy, 1 - sign))
        put(spread.at[dy], to_out, to_in, same[512:])
    for seg in range(5):
        rows = NY if seg < 4 else HY
        sums_ref[pl.ds(seg * NY, rows), :] = shifted(spread, seg)


def inner(out, into, tables):
    vmem = pl.BlockSpec(memory_space=pltpu.VMEM)
    return pl.pallas_call(
        inner_kernel,
        in_specs=[vmem, vmem, vmem],
        out_specs=vmem,
        out_shape=jax.ShapeDtypeStruct((FINE + HY, 256), F32),
        scratch_shapes=[
            pltpu.VMEM((FINE + HY, 768), BF16),
            pltpu.VMEM((7, SUMS + 16, 256), F32),
        ],
        compiler_params=pltpu.CompilerParams(vmem_limit_bytes=VMEM),
        cost_estimate=pl.CostEstimate(flops=3_000_000_000, bytes_accessed=6_000_000, transcendentals=0),
        name="inner",
    )(out, into, pltpu.with_memory_space_constraint(tables, pltpu.VMEM))


def outer_kernel(cross_ref, pair_ref, tables, inner_ref, fine_ref, coarse_ref, sources, spread, shuffled):
    core = core_parity()
    clear_gaps(spread)
    for at, ref in enumerate((cross_ref, pair_ref)):
        sources[at] = jnp.concatenate([slabs(ref), coarse_slab(ref)], axis=0)
    for dy in range(7):
        by_cross = dot(sources[0], operator(tables, dy, 2 * core))
        by_pair = dot(sources[1], operator(tables, dy, 2 - 2 * core))
        put(spread.at[dy], by_cross[0:256], by_pair[0:256], by_cross[256:] + by_pair[256:])
    for q in range(2):
        pz = q + core - 2 * q * core
        for px in range(2):
            seg = 2 * q + px
            done = (inner_ref[pl.ds(seg * NY, NY), :] + shifted(spread, seg)).T
            for child in range(4):
                first = (2 * px + child // 2) * 4 + 2 * pz + child % 2
                fine_ref[pl.ds(first, COEF, stride=16), :] = done[child * SLOT : child * SLOT + COEF]
    done = (inner_ref[pl.ds(FINE, HY), :] + shifted(spread, 4)).T
    for child in range(4):
        shuffled[pl.ds(child, COEF, stride=4), :] = done[child * SLOT : child * SLOT + COEF]
    coarse_ref[...] = shuffled[...].reshape(COEF, 2, 2, HY)


def outer(cross, pair, tables, sums):
    vmem = pl.BlockSpec(memory_space=pltpu.VMEM)
    return pl.pallas_call(
        outer_kernel,
        in_specs=[vmem, vmem, vmem, vmem],
        out_specs=[vmem, vmem],
        out_shape=[
            jax.ShapeDtypeStruct((16 * COEF, NY), F32),
            jax.ShapeDtypeStruct((COEF, 2, 2, HY), F32),
        ],
        scratch_shapes=[
            pltpu.VMEM((2, 256 + HY, 768), BF16),
            pltpu.VMEM((7, SUMS + 16, 256), F32),
            pltpu.VMEM((4 * COEF, HY), F32),
        ],
        compiler_params=pltpu.CompilerParams(vmem_limit_bytes=VMEM),
        cost_estimate=pl.CostEstimate(flops=2_000_000_000, bytes_accessed=5_000_000, transcendentals=0),
        name="outer",
    )(cross, pair, pltpu.with_memory_space_constraint(tables, pltpu.VMEM), sums)


def exchange(array, axis, start):
    count = lax.axis_size(axis)
    there = [(i, i + 1) for i in range(start, count - 1, 2)]
    return lax.ppermute(array, axis, there + [(j, i) for i, j in there])


def shards(multipoles, translate_far, translate_up):
    a = exchange(multipoles, "wide", 0)
    b = exchange(multipoles, "wide", 1)
    flat = lambda brick: brick.reshape(16 * COEF, NY)
    up = translate_up.transpose(1, 0, 2).reshape(8 * COEF, COEF)
    tables, *own, parents = early(translate_far, flat(multipoles), up)
    out, into = pack(flat(a), flat(b), own)
    cross = exchange(out, "narrow", 1)
    pair = exchange(into, "narrow", 0)
    sums = inner(out, into, tables)
    fine, coarse = outer(cross, pair, tables, sums)
    return fine.reshape(COEF, 4, 4, NY), parents, coarse


def solution(mesh):
    return jax.shard_map(
        shards,
        mesh=mesh,
        in_specs=(P(None, "wide", "narrow", None), P(), P()),
        out_specs=(
            P(None, "wide", "narrow", None),
            P(None, "wide", "narrow", None),
            P(None, "wide", "narrow", None),
        ),
        check_vma=False,
    )
```

time: 39.8 us -> 27.1 us (0.68)
  the two profiles are of different devices: /device:TPU:113 before, /device:TPU:131 now
where the time goes in v1:
time: 27.1 us; the launch traced here: 27 us
  Pallas kernels  12.2 us (45%)
  starting transfers between devices  9.69 us (36%)
  waiting for transfers between devices  4.42 us (16%)
  between operations  0.69 us (3%)
    ppermute x4, starting transfers between devices, exchange(): return lax.ppermute(array, axis, there + [(j, i) for i, j in there])  9.69 us
    pallas_call x1, Pallas kernels, early(): pl.pallas_call(early_kernel, in_specs=[hbm] * 3, out_specs=[vmem] * 5, ou...  5.4 us
    ppermute x4, waiting for transfers between devices, exchange(): return lax.ppermute(array, axis, there + [(j, i) for i, j in there])  4.42 us
    pallas_call x1, Pallas kernels, inner(): pl.pallas_call(inner_kernel, in_specs=[vmem, vmem, vmem], out_specs=vmem,...  3 us
    pallas_call x1, Pallas kernels, outer(): pl.pallas_call(outer_kernel, in_specs=[vmem, vmem, vmem, vmem], out_specs...  2.88 us
    pallas_call x1, Pallas kernels, pack(): pl.pallas_call(pack_kernel, in_specs=[vmem] * 5, out_specs=[vmem] * 2, ou...  0.93 us
  transfers between devices with their start and end apart: 4, of which 2 were waited for; matrix products, arithmetic and copies ran while one was open for 0% of the time, Pallas kernels for 31%

profile of v1, /device:TPU:131, one launch (start us, length us, event | category | flops | bytes accessed | tf_op | source)
XLA Modules:
  0.0 27.0 jit_solution(10516950542056667376)
XLA Ops:
  0.6 1.4 %collective-permute-start = (bf16[49,4,4,128]{3,2,1,0:T(4,128)(2,1)}, bf16[49,4,4,128]{3,2,1,0:T(4,128)(2,1)S(1)}, u32[]{:S(2)}, u32[]{:S(2)}) collective-permute-start(bf16[49,4,4,128]{3,2,1,0:T(4,128)(2,1)} %param.3), channel_id=1, source_target_pairs={{0,8},{16,24},{32,40},{48,56},{64,72},{80,88},{96,104},{112,120},{... | collective-permute-start | bytes 602120 | tf_op jit(solution)/shard_map/ppermute | solution.py:314
  2.0 3.3 %collective-permute-start.1 = (bf16[49,4,4,128]{3,2,1,0:T(4,128)(2,1)}, bf16[49,4,4,128]{3,2,1,0:T(4,128)(2,1)S(1)}, u32[]{:S(2)}, u32[]{:S(2)}) collective-permute-start(bf16[49,4,4,128]{3,2,1,0:T(4,128)(2,1)} %param.3), channel_id=1, source_target_pairs={{8,16},{24,32},{40,48},{56,64},{72,80},{88,96},{104,112},{120,128}... | collective-permute-start | bytes 602120 | tf_op jit(solution)/shard_map/ppermute | solution.py:314
  5.4 5.4 %early.1 = (bf16[7,3,7,128,128]{4,3,2,1,0:T(8,128)(2,1)S(1)}, bf16[512,256]{1,0:T(8,128)(2,1)S(1)}, bf16[64,256]{1,0:T(8,128)(2,1)S(1)}, bf16[256,128]{1,0:T(8,128)(2,1)S(1)}, bf16[49,2,2,64]{3,2,1,0:T(2,128)(2,1)}) custom-call(bf16[7,7,7,49,49]{4,3,2,1,0:T(8,128)(2,1)} %far_hbm.1, bf16[784,128]{1,0:T(8,128)(2,1)} %bitcast.9, bf16[392,49]{1,0:T(8,128)(2,1)} %bitcast.10), custom_call_target="tpu_custom_call" | custom-call | bytes 10000000 | tf_op jit(solution)/shard_map/early/pallas_call | solution.py:119
  10.8 0.0 collective-permute-done
  10.8 2.2 %collective-permute-done.1 = bf16[49,4,4,128]{3,2,1,0:T(4,128)(2,1)S(1)} collective-permute-done((bf16[49,4,4,128]{3,2,1,0:T(4,128)(2,1)}, bf16[49,4,4,128]{3,2,1,0:T(4,128)(2,1)S(1)}, u32[]{:S(2)}, u32[]{:S(2)}) %collective-permute-start.1) | collective-permute-done | bytes 200736 | tf_op jit(solution)/shard_map/ppermute | solution.py:314
  13.0 0.9 %pack.1 = (bf16[704,256]{1,0:T(8,128)(2,1)S(1)}, bf16[704,256]{1,0:T(8,128)(2,1)S(1)}) custom-call(bf16[784,128]{1,0:T(8,128)(2,1)S(1)} %bitcast.7, bf16[784,128]{1,0:T(8,128)(2,1)S(1)} %bitcast.8, bf16[512,256]{1,0:T(8,128)(2,1)S(1)} %get-tuple-element.12.slabs_ref, bf16[64,256]{1,0:T(8,128)(2,1)S(1)} %get-tuple-element.13.coarse_ref, ...), custom_call_target="tpu_custom_call" | custom-call | tf_op jit(solution)/shard_map/pack/pallas_call | solution.py:174
  13.9 4.9 %collective-permute-start.2 = (bf16[704,256]{1,0:T(8,128)(2,1)S(1)}, bf16[704,256]{1,0:T(8,128)(2,1)S(1)}, u32[]{:S(2)}, u32[]{:S(2)}) collective-permute-start(bf16[704,256]{1,0:T(8,128)(2,1)S(1)} %get-tuple-element.15.out_ref), channel_id=1, source_target_pairs={{1,2},{3,4},{5,6},{2,1},{4,3},{6,5},{9,10},{11,12},{13,14},{10,9},... | collective-permute-start | bytes 1081352 | tf_op jit(solution)/shard_map/ppermute | solution.py:314
  18.8 0.1 collective-permute-start.3
  18.9 3.0 %inner.1.inner_ref = f32[576,256]{1,0:T(8,128)S(1)} custom-call(bf16[704,256]{1,0:T(8,128)(2,1)S(1)} %get-tuple-element.15.out_ref, bf16[704,256]{1,0:T(8,128)(2,1)S(1)} %get-tuple-element.16.in_ref, bf16[7,3,7,128,128]{4,3,2,1,0:T(8,128)(2,1)S(1)} %get-tuple-element.17.tables), custom_call_target="tpu_custom_call" | custom-call | flops 3000000000 | bytes 6000000 | tf_op jit(solution)/shard_map/inner/pallas_call | solution.py:252
  21.9 2.2 %collective-permute-done.2.cross_ref = bf16[704,256]{1,0:T(8,128)(2,1)S(1)} collective-permute-done((bf16[704,256]{1,0:T(8,128)(2,1)S(1)}, bf16[704,256]{1,0:T(8,128)(2,1)S(1)}, u32[]{:S(2)}, u32[]{:S(2)}) %collective-permute-start.2) | collective-permute-done | bytes 360480 | tf_op jit(solution)/shard_map/ppermute | solution.py:314
  24.1 0.0 collective-permute-done.3.pair_ref
  24.1 2.9 %outer.1 = (f32[784,128]{1,0:T(8,128)}, f32[49,2,2,64]{3,2,1,0:T(2,128)}) custom-call(bf16[704,256]{1,0:T(8,128)(2,1)S(1)} %collective-permute-done.2.cross_ref, bf16[704,256]{1,0:T(8,128)(2,1)S(1)} %collective-permute-done.3.pair_ref, bf16[7,3,7,128,128]{4,3,2,1,0:T(8,128)(2,1)S(1)} %get-tuple-element.17.tables, f32[576,256]{1,0:T(8,128)S(1)} %inner.1.inner_ref), custom_call_target="tpu_custom_call" | custom-call | flops 2000000000 | bytes 5000000 | tf_op jit(solution)/shard_map/outer/pallas_call | solution.py:292
Async XLA Ops:
  0.6 10.1 %collective-permute-start = (bf16[49,4,4,128]{3,2,1,0:T(4,128)(2,1)}, bf16[49,4,4,128]{3,2,1,0:T(4,128)(2,1)S(1)}, u32[]{:S(2)}, u32[]{:S(2)}) collective-permute-start(bf16[49,4,4,128]{3,2,1,0:T(4,128)(2,1)} %param.3), channel_id=1, source_target_pairs={{0,8},{16,24},{32,40},{48,56},{64,72},{80,88},{96,104},{112,120},{... | collective-permute-start | bytes 602120 | tf_op jit(solution)/shard_map/ppermute | solution.py:314
  2.0 11.0 %collective-permute-start.1 = (bf16[49,4,4,128]{3,2,1,0:T(4,128)(2,1)}, bf16[49,4,4,128]{3,2,1,0:T(4,128)(2,1)S(1)}, u32[]{:S(2)}, u32[]{:S(2)}) collective-permute-start(bf16[49,4,4,128]{3,2,1,0:T(4,128)(2,1)} %param.3), channel_id=1, source_target_pairs={{8,16},{24,32},{40,48},{56,64},{72,80},{88,96},{104,112},{120,128}... | collective-permute-start | bytes 602120 | tf_op jit(solution)/shard_map/ppermute | solution.py:314
  13.9 10.2 %collective-permute-start.2 = (bf16[704,256]{1,0:T(8,128)(2,1)S(1)}, bf16[704,256]{1,0:T(8,128)(2,1)S(1)}, u32[]{:S(2)}, u32[]{:S(2)}) collective-permute-start(bf16[704,256]{1,0:T(8,128)(2,1)S(1)} %get-tuple-element.15.out_ref), channel_id=1, source_target_pairs={{1,2},{3,4},{5,6},{2,1},{4,3},{6,5},{9,10},{11,12},{13,14},{10,9},... | collective-permute-start | bytes 1081352 | tf_op jit(solution)/shard_map/ppermute | solution.py:314
  18.8 5.3 %collective-permute-start.3 = (bf16[704,256]{1,0:T(8,128)(2,1)S(1)}, bf16[704,256]{1,0:T(8,128)(2,1)S(1)}, u32[]{:S(2)}, u32[]{:S(2)}) collective-permute-start(bf16[704,256]{1,0:T(8,128)(2,1)S(1)} %get-tuple-element.16.in_ref), channel_id=1, source_target_pairs={{0,1},{2,3},{4,5},{6,7},{1,0},{3,2},{5,4},{7,6},{8,9},{10,11},{12,... | collective-permute-start | bytes 1081352 | tf_op jit(solution)/shard_map/ppermute | solution.py:314

commit v2 on v1

--- a/solution.py
+++ b/solution.py
@@ -15,7 +15,6 @@
 FINE = 4 * NY
 ROWS = FINE + 3 * HY
 SEG = NY + 8
-SUMS = 4 * SEG + HY
 VMEM = 20 * 2**20
 
 
@@ -144,7 +143,7 @@
     )(*[pltpu.with_memory_space_constraint(x, pltpu.HBM) for x in (far, own, up)])
 
 
-def pack_kernel(a_ref, b_ref, slabs_ref, coarse_ref, pairs_ref, out_ref, in_ref, bricks, halves):
+def pack_kernel(b_ref, a_ref, slabs_ref, coarse_ref, pairs_ref, out_ref, in_ref, bricks, halves):
     odd, core = lax.rem(lax.axis_index("wide"), 2), core_parity()
     bricks[:, pl.ds(16 * COEF, 16 * (SLOT - COEF)), :] = jnp.zeros((2, 16 * (SLOT - COEF), NY), F32)
     bricks[1 - odd, pl.ds(0, 16 * COEF), :] = a_ref[...].astype(F32)
@@ -202,14 +201,13 @@
     return jnp.concatenate([ref[pl.ds(FINE + x * HY, HY), :] for x in range(3)], axis=1)
 
 
-def clear_gaps(spread):
-    for seg in range(5):
+def clear_gaps(spread, count):
+    for seg in range(count + 1):
         spread[:, pl.ds(seg * SEG, 8), :] = jnp.zeros((7, 8, 256), F32)
-    spread[:, pl.ds(8 + 4 * SEG + HY, 8), :] = jnp.zeros((7, 8, 256), F32)
-
-
-def shifted(spread, seg):
-    rows = NY if seg < 4 else HY
+    spread[:, pl.ds(8 + count * SEG + HY, 8), :] = jnp.zeros((7, 8, 256), F32)
+
+
+def shifted(spread, seg, rows):
     even = lax.broadcasted_iota(jnp.int32, (rows, 256), 0) % 2 == 0
     total = None
     for dy in range(7):
@@ -222,90 +220,97 @@
     return total
 
 
-def put(spread, fine_out, fine_in, coarse):
-    for px in range(2):
-        spread[pl.ds(8 + px * SEG, NY), :] = fine_out[px * NY : (px + 1) * NY]
-        spread[pl.ds(8 + (2 + px) * SEG, NY), :] = fine_in[px * NY : (px + 1) * NY]
-    spread[pl.ds(8 + 4 * SEG, HY), :] = coarse
-
-
-def inner_kernel(out_ref, in_ref, tables, sums_ref, sources, spread):
-    sign = 1 - 2 * core_parity()
-    clear_gaps(spread)
+def put(spread, fine, coarse):
+    for seg in range(fine.shape[0] // NY):
+        spread[pl.ds(8 + seg * SEG, NY), :] = fine[seg * NY : (seg + 1) * NY]
+    spread[pl.ds(8 + (fine.shape[0] // NY) * SEG, HY), :] = coarse
+
+
+def finish(fine_ref, done, px, pz):
+    for child in range(4):
+        first = (2 * px + child // 2) * 4 + 2 * pz + child % 2
+        fine_ref[pl.ds(first, COEF, stride=16), :] = done[child * SLOT : child * SLOT + COEF]
+
+
+def inner_kernel(out_ref, in_ref, pair_ref, tables, part_ref, sums_ref, sources, beyond, spread):
+    core = core_parity()
+    sign = 1 - 2 * core
+    clear_gaps(spread, 4)
     sources[...] = jnp.concatenate([slabs(out_ref), slabs(in_ref), coarse_slab(out_ref)], axis=0)
+    beyond[...] = jnp.concatenate([slabs(pair_ref), coarse_slab(pair_ref)], axis=0)
     for dy in range(7):
         if 2 <= dy <= 4:
             beside = jnp.concatenate([sources[:, 0:256], sources[:, 512:768]], axis=1)
             same = dot(beside, operator(tables, dy, 1, True))
         else:
             same = dot(sources[...], operator(tables, dy, 1))
-        to_out = same[0:256] + dot(sources[256:512, :], operator(tables, dy, 1 + sign))
-        to_in = same[256:512] + dot(sources[0:256, :], operator(tables, dy, 1 - sign))
-        put(spread.at[dy], to_out, to_in, same[512:])
-    for seg in range(5):
-        rows = NY if seg < 4 else HY
-        sums_ref[pl.ds(seg * NY, rows), :] = shifted(spread, seg)
-
-
-def inner(out, into, tables):
+        ahead = dot(jnp.concatenate([sources[256:512, :], beyond[...]], axis=0), operator(tables, dy, 1 + sign))
+        behind = dot(sources[0:256, :], operator(tables, dy, 1 - sign))
+        to_out = same[0:256] + ahead[0:256]
+        to_in = same[256:512] + ahead[256:512] + behind
+        put(spread.at[dy], jnp.concatenate([to_out, to_in], axis=0), same[512:] + ahead[512:])
+    for seg in range(2):
+        sums_ref[pl.ds(seg * NY, NY), :] = shifted(spread, seg, NY)
+        finish(part_ref, shifted(spread, 2 + seg, NY).T, seg, 1 - core)
+    sums_ref[pl.ds(2 * NY, HY), :] = shifted(spread, 4, HY)
+
+
+def inner(out, into, pair, tables):
     vmem = pl.BlockSpec(memory_space=pltpu.VMEM)
     return pl.pallas_call(
         inner_kernel,
-        in_specs=[vmem, vmem, vmem],
-        out_specs=vmem,
-        out_shape=jax.ShapeDtypeStruct((FINE + HY, 256), F32),
+        in_specs=[vmem] * 4,
+        out_specs=[vmem] * 2,
+        out_shape=[
+            jax.ShapeDtypeStruct((16 * COEF, NY), F32),
+            jax.ShapeDtypeStruct((2 * NY + HY, 256), F32),
+        ],
         scratch_shapes=[
             pltpu.VMEM((FINE + HY, 768), BF16),
-            pltpu.VMEM((7, SUMS + 16, 256), F32),
+            pltpu.VMEM((2 * NY + HY, 768), BF16),
+            pltpu.VMEM((7, 4 * SEG + HY + 16, 256), F32),
         ],
         compiler_params=pltpu.CompilerParams(vmem_limit_bytes=VMEM),
         cost_estimate=pl.CostEstimate(flops=3_000_000_000, bytes_accessed=6_000_000, transcendentals=0),
         name="inner",
-    )(out, into, pltpu.with_memory_space_constraint(tables, pltpu.VMEM))
-
-
-def outer_kernel(cross_ref, pair_ref, tables, inner_ref, fine_ref, coarse_ref, sources, spread, shuffled):
+    )(out, into, pair, pltpu.with_memory_space_constraint(tables, pltpu.VMEM))
+
+
+def outer_kernel(cross_ref, tables, part_ref, sums_ref, fine_ref, coarse_ref, sources, spread, shuffled):
     core = core_parity()
-    clear_gaps(spread)
-    for at, ref in enumerate((cross_ref, pair_ref)):
-        sources[at] = jnp.concatenate([slabs(ref), coarse_slab(ref)], axis=0)
+    clear_gaps(spread, 2)
+    sources[...] = jnp.concatenate([slabs(cross_ref), coarse_slab(cross_ref)], axis=0)
     for dy in range(7):
-        by_cross = dot(sources[0], operator(tables, dy, 2 * core))
-        by_pair = dot(sources[1], operator(tables, dy, 2 - 2 * core))
-        put(spread.at[dy], by_cross[0:256], by_pair[0:256], by_cross[256:] + by_pair[256:])
-    for q in range(2):
-        pz = q + core - 2 * q * core
-        for px in range(2):
-            seg = 2 * q + px
-            done = (inner_ref[pl.ds(seg * NY, NY), :] + shifted(spread, seg)).T
-            for child in range(4):
-                first = (2 * px + child // 2) * 4 + 2 * pz + child % 2
-                fine_ref[pl.ds(first, COEF, stride=16), :] = done[child * SLOT : child * SLOT + COEF]
-    done = (inner_ref[pl.ds(FINE, HY), :] + shifted(spread, 4)).T
+        found = dot(sources[...], operator(tables, dy, 2 * core))
+        put(spread.at[dy], found[0:256], found[256:])
+    fine_ref[...] = part_ref[...]
+    for seg in range(2):
+        finish(fine_ref, (sums_ref[pl.ds(seg * NY, NY), :] + shifted(spread, seg, NY)).T, seg, core)
+    done = (sums_ref[pl.ds(2 * NY, HY), :] + shifted(spread, 2, HY)).T
     for child in range(4):
         shuffled[pl.ds(child, COEF, stride=4), :] = done[child * SLOT : child * SLOT + COEF]
     coarse_ref[...] = shuffled[...].reshape(COEF, 2, 2, HY)
 
 
-def outer(cross, pair, tables, sums):
+def outer(cross, tables, part, sums):
     vmem = pl.BlockSpec(memory_space=pltpu.VMEM)
     return pl.pallas_call(
         outer_kernel,
-        in_specs=[vmem, vmem, vmem, vmem],
+        in_specs=[vmem] * 4,
         out_specs=[vmem, vmem],
         out_shape=[
             jax.ShapeDtypeStruct((16 * COEF, NY), F32),
             jax.ShapeDtypeStruct((COEF, 2, 2, HY), F32),
         ],
         scratch_shapes=[
-            pltpu.VMEM((2, 256 + HY, 768), BF16),
-            pltpu.VMEM((7, SUMS + 16, 256), F32),
+            pltpu.VMEM((2 * NY + HY, 768), BF16),
+            pltpu.VMEM((7, 2 * SEG + HY + 16, 256), F32),
             pltpu.VMEM((4 * COEF, HY), F32),
         ],
         compiler_params=pltpu.CompilerParams(vmem_limit_bytes=VMEM),
-        cost_estimate=pl.CostEstimate(flops=2_000_000_000, bytes_accessed=5_000_000, transcendentals=0),
+        cost_estimate=pl.CostEstimate(flops=1_000_000_000, bytes_accessed=5_000_000, transcendentals=0),
         name="outer",
-    )(cross, pair, pltpu.with_memory_space_constraint(tables, pltpu.VMEM), sums)
+    )(cross, pltpu.with_memory_space_constraint(tables, pltpu.VMEM), part, sums)
 
 
 def exchange(array, axis, start):
@@ -315,16 +320,16 @@
 
 
 def shards(multipoles, translate_far, translate_up):
+    b = exchange(multipoles, "wide", 1)
     a = exchange(multipoles, "wide", 0)
-    b = exchange(multipoles, "wide", 1)
     flat = lambda brick: brick.reshape(16 * COEF, NY)
     up = translate_up.transpose(1, 0, 2).reshape(8 * COEF, COEF)
     tables, *own, parents = early(translate_far, flat(multipoles), up)
-    out, into = pack(flat(a), flat(b), own)
+    out, into = pack(flat(b), flat(a), own)
+    pair = exchange(into, "narrow", 0)
     cross = exchange(out, "narrow", 1)
-    pair = exchange(into, "narrow", 0)
-    sums = inner(out, into, tables)
-    fine, coarse = outer(cross, pair, tables, sums)
+    part, sums = inner(out, into, pair, tables)
+    fine, coarse = outer(cross, tables, part, sums)
     return fine.reshape(COEF, 4, 4, NY), parents, coarse
 
 

time: 27.1 us -> 25.3 us (0.934)
  waiting for transfers between devices: 4.42 us -> 2.94 us
  starting transfers between devices: 9.69 us -> 9.24 us
    ppermute x4, waiting for transfers between devices: 4.42 us -> 2.94 us  [exchange(): return lax.ppermute(array, axis, there + [(j, i) for i, j in there])]
    ppermute x4, starting transfers between devices: 9.69 us -> 9.24 us  [exchange(): return lax.ppermute(array, axis, there + [(j, i) for i, j in there])]
  transfers between devices with their start and end apart: 4 -> 4, of which waited for: 2 -> 2; matrix products, arithmetic and copies ran while one was open for 0% -> 0% of each run, Pallas kernels for 31% -> 37%
where the time goes in v2:
time: 25.3 us; the launch traced here: 25.2 us
  Pallas kernels  12.3 us (49%)
  starting transfers between devices  9.24 us (37%)
  waiting for transfers between devices  2.94 us (12%)
  between operations  0.68 us (3%)
    ppermute x4, starting transfers between devices, exchange(): return lax.ppermute(array, axis, there + [(j, i) for i, j in there])  9.24 us
    pallas_call x1, Pallas kernels, early(): pl.pallas_call(early_kernel, in_specs=[hbm] * 3, out_specs=[vmem] * 5, ou...  5.4 us
    pallas_call x1, Pallas kernels, inner(): pl.pallas_call(inner_kernel, in_specs=[vmem] * 4, out_specs=[vmem] * 2, o...  4.04 us
    ppermute x4, waiting for transfers between devices, exchange(): return lax.ppermute(array, axis, there + [(j, i) for i, j in there])  2.94 us
    pallas_call x1, Pallas kernels, outer(): pl.pallas_call(outer_kernel, in_specs=[vmem] * 4, out_specs=[vmem, vmem],...  1.95 us
    pallas_call x1, Pallas kernels, pack(): pl.pallas_call(pack_kernel, in_specs=[vmem] * 5, out_specs=[vmem] * 2, ou...  0.93 us
  transfers between devices with their start and end apart: 4, of which 2 were waited for; matrix products, arithmetic and copies ran while one was open for 0% of the time, Pallas kernels for 37%

profile of v2, /device:TPU:131, one launch (start us, length us, event | category | flops | bytes accessed | tf_op | source)
XLA Modules:
  0.0 25.2 jit_solution(13338270294619753674)
XLA Ops:
  0.6 4.2 %collective-permute-start = (bf16[49,4,4,128]{3,2,1,0:T(4,128)(2,1)}, bf16[49,4,4,128]{3,2,1,0:T(4,128)(2,1)S(1)}, u32[]{:S(2)}, u32[]{:S(2)}) collective-permute-start(bf16[49,4,4,128]{3,2,1,0:T(4,128)(2,1)} %param.3), channel_id=1, source_target_pairs={{8,16},{24,32},{40,48},{56,64},{72,80},{88,96},{104,112},{120,128}... | collective-permute-start | bytes 602120 | tf_op jit(solution)/shard_map/ppermute | solution.py:319
  4.8 0.4 %collective-permute-start.1 = (bf16[49,4,4,128]{3,2,1,0:T(4,128)(2,1)}, bf16[49,4,4,128]{3,2,1,0:T(4,128)(2,1)S(1)}, u32[]{:S(2)}, u32[]{:S(2)}) collective-permute-start(bf16[49,4,4,128]{3,2,1,0:T(4,128)(2,1)} %param.3), channel_id=1, source_target_pairs={{0,8},{16,24},{32,40},{48,56},{64,72},{80,88},{96,104},{112,120},{... | collective-permute-start | bytes 602120 | tf_op jit(solution)/shard_map/ppermute | solution.py:319
  5.2 5.4 %early.1 = (bf16[7,3,7,128,128]{4,3,2,1,0:T(8,128)(2,1)S(1)}, bf16[512,256]{1,0:T(8,128)(2,1)S(1)}, bf16[64,256]{1,0:T(8,128)(2,1)S(1)}, bf16[256,128]{1,0:T(8,128)(2,1)S(1)}, bf16[49,2,2,64]{3,2,1,0:T(2,128)(2,1)}) custom-call(bf16[7,7,7,49,49]{4,3,2,1,0:T(8,128)(2,1)} %far_hbm.1, bf16[784,128]{1,0:T(8,128)(2,1)} %bitcast.9, bf16[392,49]{1,0:T(8,128)(2,1)} %bitcast.10), custom_call_target="tpu_custom_call" | custom-call | bytes 10000000 | tf_op jit(solution)/shard_map/early/pallas_call | solution.py:118
  10.6 1.3 %collective-permute-done = bf16[49,4,4,128]{3,2,1,0:T(4,128)(2,1)S(1)} collective-permute-done((bf16[49,4,4,128]{3,2,1,0:T(4,128)(2,1)}, bf16[49,4,4,128]{3,2,1,0:T(4,128)(2,1)S(1)}, u32[]{:S(2)}, u32[]{:S(2)}) %collective-permute-start) | collective-permute-done | bytes 200736 | tf_op jit(solution)/shard_map/ppermute | solution.py:319
  11.9 0.0 collective-permute-done.1
  11.9 0.9 %pack.1 = (bf16[704,256]{1,0:T(8,128)(2,1)S(1)}, bf16[704,256]{1,0:T(8,128)(2,1)S(1)}) custom-call(bf16[784,128]{1,0:T(8,128)(2,1)S(1)} %bitcast.7, bf16[784,128]{1,0:T(8,128)(2,1)S(1)} %bitcast.8, bf16[512,256]{1,0:T(8,128)(2,1)S(1)} %get-tuple-element.14.slabs_ref, bf16[64,256]{1,0:T(8,128)(2,1)S(1)} %get-tuple-element.15.coarse_ref, ...), custom_call_target="tpu_custom_call" | custom-call | tf_op jit(solution)/shard_map/pack/pallas_call | solution.py:173
  12.9 1.6 %collective-permute-start.3 = (bf16[704,256]{1,0:T(8,128)(2,1)S(1)}, bf16[704,256]{1,0:T(8,128)(2,1)S(1)}, u32[]{:S(2)}, u32[]{:S(2)}) collective-permute-start(bf16[704,256]{1,0:T(8,128)(2,1)S(1)} %get-tuple-element.19.in_ref), channel_id=1, source_target_pairs={{0,1},{2,3},{4,5},{6,7},{1,0},{3,2},{5,4},{7,6},{8,9},{10,11},{12,... | collective-permute-start | bytes 1081352 | tf_op jit(solution)/shard_map/ppermute | solution.py:319
  14.5 3.0 %collective-permute-start.2 = (bf16[704,256]{1,0:T(8,128)(2,1)S(1)}, bf16[704,256]{1,0:T(8,128)(2,1)S(1)}, u32[]{:S(2)}, u32[]{:S(2)}) collective-permute-start(bf16[704,256]{1,0:T(8,128)(2,1)S(1)} %get-tuple-element.17.out_ref), channel_id=1, source_target_pairs={{1,2},{3,4},{5,6},{2,1},{4,3},{6,5},{9,10},{11,12},{13,14},{10,9},... | collective-permute-start | bytes 1081352 | tf_op jit(solution)/shard_map/ppermute | solution.py:319
  17.5 0.0 collective-permute-done.3.pair_ref
  17.5 4.0 %inner.1 = (f32[784,128]{1,0:T(8,128)S(1)}, f32[320,256]{1,0:T(8,128)S(1)}) custom-call(bf16[704,256]{1,0:T(8,128)(2,1)S(1)} %get-tuple-element.17.out_ref, bf16[704,256]{1,0:T(8,128)(2,1)S(1)} %get-tuple-element.19.in_ref, bf16[704,256]{1,0:T(8,128)(2,1)S(1)} %collective-permute-done.3.pair_ref, bf16[7,3,7,128,128]{4,3,2,1,0:T(8,128)(2,1)S(1)} %get-tuple-element.18.tables), custom_call_target="tpu_custom_call" | custom-call | flops 3000000000 | bytes 6000000 | tf_op jit(solution)/shard_map/inner/pallas_call | solution.py:260
  21.6 1.7 %collective-permute-done.2.cross_ref = bf16[704,256]{1,0:T(8,128)(2,1)S(1)} collective-permute-done((bf16[704,256]{1,0:T(8,128)(2,1)S(1)}, bf16[704,256]{1,0:T(8,128)(2,1)S(1)}, u32[]{:S(2)}, u32[]{:S(2)}) %collective-permute-start.2) | collective-permute-done | bytes 360480 | tf_op jit(solution)/shard_map/ppermute | solution.py:319
  23.2 2.0 %outer.1 = (f32[784,128]{1,0:T(8,128)}, f32[49,2,2,64]{3,2,1,0:T(2,128)}) custom-call(bf16[704,256]{1,0:T(8,128)(2,1)S(1)} %collective-permute-done.2.cross_ref, bf16[7,3,7,128,128]{4,3,2,1,0:T(8,128)(2,1)S(1)} %get-tuple-element.18.tables, f32[784,128]{1,0:T(8,128)S(1)} %get-tuple-element.20.part_ref, f32[320,256]{1,0:T(8,128)S(1)} %get-tuple-element.21.sums_ref), custom_call_target="tpu_custom_call" | custom-call | flops 1000000000 | bytes 5000000 | tf_op jit(solution)/shard_map/outer/pallas_call | solution.py:297
Async XLA Ops:
  0.6 11.3 %collective-permute-start = (bf16[49,4,4,128]{3,2,1,0:T(4,128)(2,1)}, bf16[49,4,4,128]{3,2,1,0:T(4,128)(2,1)S(1)}, u32[]{:S(2)}, u32[]{:S(2)}) collective-permute-start(bf16[49,4,4,128]{3,2,1,0:T(4,128)(2,1)} %param.3), channel_id=1, source_target_pairs={{8,16},{24,32},{40,48},{56,64},{72,80},{88,96},{104,112},{120,128}... | collective-permute-start | bytes 602120 | tf_op jit(solution)/shard_map/ppermute | solution.py:319
  4.8 7.1 %collective-permute-start.1 = (bf16[49,4,4,128]{3,2,1,0:T(4,128)(2,1)}, bf16[49,4,4,128]{3,2,1,0:T(4,128)(2,1)S(1)}, u32[]{:S(2)}, u32[]{:S(2)}) collective-permute-start(bf16[49,4,4,128]{3,2,1,0:T(4,128)(2,1)} %param.3), channel_id=1, source_target_pairs={{0,8},{16,24},{32,40},{48,56},{64,72},{80,88},{96,104},{112,120},{... | collective-permute-start | bytes 602120 | tf_op jit(solution)/shard_map/ppermute | solution.py:319
  12.9 4.7 %collective-permute-start.3 = (bf16[704,256]{1,0:T(8,128)(2,1)S(1)}, bf16[704,256]{1,0:T(8,128)(2,1)S(1)}, u32[]{:S(2)}, u32[]{:S(2)}) collective-permute-start(bf16[704,256]{1,0:T(8,128)(2,1)S(1)} %get-tuple-element.19.in_ref), channel_id=1, source_target_pairs={{0,1},{2,3},{4,5},{6,7},{1,0},{3,2},{5,4},{7,6},{8,9},{10,11},{12,... | collective-permute-start | bytes 1081352 | tf_op jit(solution)/shard_map/ppermute | solution.py:319
  14.5 8.7 %collective-permute-start.2 = (bf16[704,256]{1,0:T(8,128)(2,1)S(1)}, bf16[704,256]{1,0:T(8,128)(2,1)S(1)}, u32[]{:S(2)}, u32[]{:S(2)}) collective-permute-start(bf16[704,256]{1,0:T(8,128)(2,1)S(1)} %get-tuple-element.17.out_ref), channel_id=1, source_target_pairs={{1,2},{3,4},{5,6},{2,1},{4,3},{6,5},{9,10},{11,12},{13,14},{10,9},... | collective-permute-start | bytes 1081352 | tf_op jit(solution)/shard_map/ppermute | solution.py:319

commit v3 on v2

--- a/solution.py
+++ b/solution.py
@@ -14,6 +14,8 @@
 HY = 64
 FINE = 4 * NY
 ROWS = FINE + 3 * HY
+NEAR = 8 * COEF
+SIDE = 496
 SEG = NY + 8
 VMEM = 20 * 2**20
 
@@ -32,14 +34,8 @@
     return lax.rem(lax.axis_index("narrow"), 2)
 
 
-def turn(unit, bricks, brick, pair, zp):
-    cells = []
-    for cx in range(2):
-        for cz in range(2):
-            first = (2 * pair + cx) * 4 + 2 * zp + cz
-            cells.append(bricks[brick, pl.ds(first, SLOT, stride=16), :].astype(BF16))
-    cells = jnp.concatenate(cells, axis=0)
-    return lax.dot_general(unit, cells, NT, preferred_element_type=F32).astype(BF16)
+def turn(unit, cells):
+    return lax.dot_general(unit, cells.astype(BF16), NT, preferred_element_type=F32)
 
 
 def to_parents(halves, at, low):
@@ -49,47 +45,89 @@
     return jnp.where(low, first, second).astype(BF16)
 
 
-def lower_lanes():
-    return lax.broadcasted_iota(jnp.int32, (HY, 128), 1) < SLOT
-
-
-def early_kernel(
-    far_hbm, own_hbm, up_hbm, tables_ref, slabs_ref, coarse_ref, pairs_ref, par_ref,
-    far, own, up, bricks, wide, halves, shuffled, far_sems, sems,
+def own_kernel(
+    own_hbm, up_hbm, a_ref, b_ref, slabs_ref, coarse_ref,
+    own, up, brick, packed, wide, pairs, halves, message, sems,
 ):
-    def fetch(dx):
-        return pltpu.make_async_copy(far_hbm.at[dx], far.at[dx], far_sems.at[dx])
-
-    get_own = pltpu.make_async_copy(own_hbm, own, sems.at[0])
-    get_up = pltpu.make_async_copy(up_hbm, up, sems.at[1])
+    odd = lax.rem(lax.axis_index("wide"), 2)
+    get_up = pltpu.make_async_copy(up_hbm, up, sems.at[0])
+    get_own = pltpu.make_async_copy(own_hbm, own, sems.at[1])
     get_own.start()
     get_up.start()
+    pairs[...] = jnp.zeros_like(pairs)
+    brick[pl.ds(16 * COEF, 16 * (SLOT - COEF)), :] = jnp.zeros((16 * (SLOT - COEF), NY), F32)
+    unit = eye(NY)
+    low = lax.broadcasted_iota(jnp.int32, (HY, 128), 1) < SLOT
+    get_up.wait()
+    wide[...] = up[...].astype(F32)
+    for child in range(8):
+        block = wide[pl.ds(child, COEF, stride=8), :].astype(BF16)
+        pairs[pl.ds(SLOT * (child // 2), COEF), pl.ds(SLOT * (child % 2), COEF)] = block
+    get_own.wait()
+    brick[pl.ds(0, 16 * COEF), :] = own[...].astype(F32)
+    cells = [brick[pl.ds(cell, SLOT, stride=16), :] for cell in range(16)]
+    for cell in range(16):
+        packed[pl.ds(COEF * cell, SLOT), :] = cells[cell]
+    order = [(2 * px + cx) * 4 + 2 * zp + cz for px in range(2) for zp in range(2) for cx in range(2) for cz in range(2)]
+    turned = turn(unit, jnp.concatenate([cells[cell] for cell in order], axis=0)).astype(BF16)
+    parts = [turned[:, 256 * at : 256 * at + 256] for at in range(4)]
+    sums = dot(jnp.concatenate(parts, axis=0), pairs[...])
+    for at in range(4):
+        slabs_ref[pl.ds(at * NY, NY), :] = parts[at]
+        halves[at] = sums[at * NY : at * NY + NY]
+    parents = [to_parents(halves, 2 * px, low) for px in range(2)]
+    for px in range(2):
+        coarse_ref[:, pl.ds(128 * px, 128)] = parents[px]
+    turned = turn(unit, jnp.concatenate(parents, axis=0))
+    message[pl.ds(NEAR, SLOT), :] = turned[0:SLOT]
+    message[pl.ds(NEAR + COEF, SLOT), :] = turned[SLOT:128]
+    for ref, half in ((b_ref, odd), (a_ref, 1 - odd)):
+        message[pl.ds(0, NEAR), :] = packed[pl.ds(pl.multiple_of(half * NEAR, 8), NEAR), :]
+        ref[...] = message[pl.ds(0, SIDE), :].astype(BF16)
+
+
+def own_part(own, up):
+    hbm = pl.BlockSpec(memory_space=pltpu.HBM)
+    vmem = pl.BlockSpec(memory_space=pltpu.VMEM)
+    return pl.pallas_call(
+        own_kernel,
+        in_specs=[hbm] * 2,
+        out_specs=[vmem] * 4,
+        out_shape=[
+            pltpu.VMEM((SIDE, NY), BF16),
+            pltpu.VMEM((SIDE, NY), BF16),
+            pltpu.VMEM((FINE, 256), BF16),
+            pltpu.VMEM((HY, 256), BF16),
+        ],
+        scratch_shapes=[
+            pltpu.VMEM((16 * COEF, NY), BF16),
+            pltpu.VMEM((8 * COEF, COEF), BF16),
+            pltpu.VMEM((16 * SLOT, NY), F32),
+            pltpu.VMEM((16 * COEF + 16, NY), F32),
+            pltpu.VMEM((8 * COEF, COEF), F32),
+            pltpu.VMEM((256, 128), BF16),
+            pltpu.VMEM((4, NY, 128), F32),
+            pltpu.VMEM((SIDE + 16, NY), F32),
+            pltpu.SemaphoreType.DMA((2,)),
+        ],
+        compiler_params=pltpu.CompilerParams(vmem_limit_bytes=VMEM),
+        name="own_part",
+    )(*[pltpu.with_memory_space_constraint(x, pltpu.HBM) for x in (own, up)])
+
+
+def tables_kernel(far_hbm, coarse_ref, tables_ref, par_ref, far, shuffled, sems):
+    def fetch(dx):
+        return pltpu.make_async_copy(far_hbm.at[dx], far.at[dx], sems.at[dx])
+
     for dx in range(7):
         fetch(dx).start()
 
-    get_up.wait()
-    wide[...] = up[...].astype(F32)
-    pairs_ref[...] = jnp.zeros_like(pairs_ref)
-    for child in range(8):
-        block = wide[pl.ds(child, COEF, stride=8), :].astype(BF16)
-        pairs_ref[pl.ds(SLOT * (child // 2), COEF), pl.ds(SLOT * (child % 2), COEF)] = block
-    get_own.wait()
-    bricks[0, pl.ds(16 * COEF, 16 * (SLOT - COEF)), :] = jnp.zeros((16 * (SLOT - COEF), NY), F32)
-    bricks[0, pl.ds(0, 16 * COEF), :] = own[...].astype(F32)
-    unit, low = eye(NY), lower_lanes()
-    core = core_parity()
+    cells = jnp.concatenate([coarse_ref[:, pl.ds(128 * px, 128)] for px in range(2)], axis=0)
+    turned = turn(eye(NY), cells)
     for px in range(2):
-        for q in range(2):
-            zp = q + core - 2 * q * core
-            turned = turn(unit, bricks, 0, px, zp)
-            slabs_ref[pl.ds((2 * q + px) * NY, NY), :] = turned
-            halves[2 * px + zp] = dot(turned, pairs_ref[...])
-    for px in range(2):
-        parent = to_parents(halves, 2 * px, low)
-        coarse_ref[:, pl.ds(128 * px, 128)] = parent
-        turned = lax.dot_general(unit, parent, NT, preferred_element_type=F32)
         for z in range(2):
-            shuffled[pl.ds(2 * px + z, COEF, stride=4), :] = turned[z * SLOT : z * SLOT + COEF]
+            block = turned[z * SLOT : z * SLOT + COEF, px * HY : (px + 1) * HY]
+            shuffled[pl.ds(2 * px + z, COEF, stride=4), :] = block
     par_ref[...] = shuffled[...].astype(BF16).reshape(COEF, 2, 2, HY)
 
     def at_dx(dx, carry):
@@ -112,76 +150,68 @@
     lax.fori_loop(0, 7, at_dx, 0)
 
 
-def early(far, own, up):
-    hbm = pl.BlockSpec(memory_space=pltpu.HBM)
-    vmem = pl.BlockSpec(memory_space=pltpu.VMEM)
-    return pl.pallas_call(
-        early_kernel,
-        in_specs=[hbm] * 3,
-        out_specs=[vmem] * 5,
+def make_tables(far, coarse):
+    vmem = pl.BlockSpec(memory_space=pltpu.VMEM)
+    return pl.pallas_call(
+        tables_kernel,
+        in_specs=[pl.BlockSpec(memory_space=pltpu.HBM), vmem],
+        out_specs=[vmem] * 2,
         out_shape=[
             pltpu.VMEM((7, 3, 7, 128, 128), BF16),
-            pltpu.VMEM((FINE, 256), BF16),
-            pltpu.VMEM((HY, 256), BF16),
-            pltpu.VMEM((256, 128), BF16),
             jax.ShapeDtypeStruct((COEF, 2, 2, HY), BF16),
         ],
         scratch_shapes=[
             pltpu.VMEM((7, 7, 7, COEF, COEF), BF16),
-            pltpu.VMEM((16 * COEF, NY), BF16),
-            pltpu.VMEM((8 * COEF, COEF), BF16),
-            pltpu.VMEM((1, 16 * SLOT, NY), F32),
-            pltpu.VMEM((8 * COEF, COEF), F32),
-            pltpu.VMEM((4, NY, 128), F32),
             pltpu.VMEM((4 * COEF, HY), F32),
             pltpu.SemaphoreType.DMA((7,)),
-            pltpu.SemaphoreType.DMA((2,)),
         ],
         compiler_params=pltpu.CompilerParams(vmem_limit_bytes=VMEM),
         cost_estimate=pl.CostEstimate(flops=0, bytes_accessed=10_000_000, transcendentals=0),
-        name="early",
-    )(*[pltpu.with_memory_space_constraint(x, pltpu.HBM) for x in (far, own, up)])
-
-
-def pack_kernel(b_ref, a_ref, slabs_ref, coarse_ref, pairs_ref, out_ref, in_ref, bricks, halves):
+        name="tables",
+    )(pltpu.with_memory_space_constraint(far, pltpu.HBM), pltpu.with_memory_space_constraint(coarse, pltpu.VMEM))
+
+
+def pack_kernel(b_ref, a_ref, slabs_ref, coarse_ref, tables_ref, out_ref, in_ref, bricks):
     odd, core = lax.rem(lax.axis_index("wide"), 2), core_parity()
-    bricks[:, pl.ds(16 * COEF, 16 * (SLOT - COEF)), :] = jnp.zeros((2, 16 * (SLOT - COEF), NY), F32)
-    bricks[1 - odd, pl.ds(0, 16 * COEF), :] = a_ref[...].astype(F32)
-    bricks[odd, pl.ds(0, 16 * COEF), :] = b_ref[...].astype(F32)
-    unit, low = eye(NY), lower_lanes()
+    unit = eye(NY)
     refs = (out_ref, in_ref)
     for q in range(2):
-        refs[q][pl.ds(NY, 2 * NY), :] = slabs_ref[pl.ds(q * 2 * NY, 2 * NY), :]
+        for px in range(2):
+            row = pl.multiple_of((2 * px + q + core - 2 * q * core) * NY, NY)
+            refs[q][pl.ds((1 + px) * NY, NY), :] = slabs_ref[pl.ds(row, NY), :]
         refs[q][pl.ds(FINE + HY, HY), :] = coarse_ref[...]
-    for brick in range(2):
-        for px in range(2):
-            for q in range(2):
-                zp = q + core - 2 * q * core
-                turned = turn(unit, bricks, brick, px, zp)
-                if px == 1 - brick:
-                    refs[q][pl.ds(brick * 3 * NY, NY), :] = turned
-                halves[4 * brick + 2 * px + zp] = dot(turned, pairs_ref[...])
-    for brick in range(2):
-        for px in range(2):
-            parent = to_parents(halves, 4 * brick + 2 * px, low)
-            for ref in refs:
-                ref[pl.ds(FINE + 2 * brick * HY, HY), pl.ds(128 * px, 128)] = parent
-
-
-def pack(a, b, own):
+    for at, (side, above) in enumerate(((b_ref, odd), (a_ref, 1 - odd))):
+        brick = bricks.at[at]
+        brick[pl.ds(0, SIDE), :] = side[...].astype(F32)
+        brick[pl.ds(SIDE, 16), :] = jnp.zeros((16, NY), F32)
+        for q in range(2):
+            zp = q + core - 2 * q * core
+            cells = []
+            for cx in range(2):
+                for cz in range(2):
+                    here = [brick[pl.ds(COEF * (4 * cx + 2 * z + cz), SLOT), :] for z in range(2)]
+                    cells.append(jnp.where(zp == 0, here[0], here[1]))
+            turned = turn(unit, jnp.concatenate(cells, axis=0)).astype(BF16)
+            refs[q][pl.ds(pl.multiple_of(above * 3 * NY, NY), NY), :] = turned
+        cells = jnp.concatenate([brick[pl.ds(NEAR + COEF * z, SLOT), :] for z in range(2)], axis=0)
+        turned = turn(unit, cells).astype(BF16)
+        for ref in refs:
+            row = pl.multiple_of(FINE + above * 2 * HY, HY)
+            for px in range(2):
+                ref[pl.ds(row, HY), pl.ds(128 * px, 128)] = turned[px * HY : (px + 1) * HY]
+
+
+def pack(b, a, slabs, coarse, tables):
     vmem = pl.BlockSpec(memory_space=pltpu.VMEM)
     return pl.pallas_call(
         pack_kernel,
         in_specs=[vmem] * 5,
         out_specs=[vmem] * 2,
         out_shape=[jax.ShapeDtypeStruct((ROWS, 256), BF16)] * 2,
-        scratch_shapes=[
-            pltpu.VMEM((2, 16 * SLOT, NY), F32),
-            pltpu.VMEM((8, NY, 128), F32),
-        ],
+        scratch_shapes=[pltpu.VMEM((2, SIDE + 16, NY), F32)],
         compiler_params=pltpu.CompilerParams(vmem_limit_bytes=VMEM),
         name="pack",
-    )(a, b, *[pltpu.with_memory_space_constraint(x, pltpu.VMEM) for x in own])
+    )(b, a, *[pltpu.with_memory_space_constraint(x, pltpu.VMEM) for x in (slabs, coarse, tables)])
 
 
 def operator(tables, dy, at, skip=False):
@@ -320,17 +350,17 @@
 
 
 def shards(multipoles, translate_far, translate_up):
-    b = exchange(multipoles, "wide", 1)
-    a = exchange(multipoles, "wide", 0)
-    flat = lambda brick: brick.reshape(16 * COEF, NY)
     up = translate_up.transpose(1, 0, 2).reshape(8 * COEF, COEF)
-    tables, *own, parents = early(translate_far, flat(multipoles), up)
-    out, into = pack(flat(b), flat(a), own)
+    to_a, to_b, slabs, coarse = own_part(multipoles.reshape(16 * COEF, NY), up)
+    b = exchange(to_b, "wide", 1)
+    a = exchange(to_a, "wide", 0)
+    tables, parents = make_tables(translate_far, coarse)
+    out, into = pack(b, a, slabs, coarse, tables)
     pair = exchange(into, "narrow", 0)
     cross = exchange(out, "narrow", 1)
     part, sums = inner(out, into, pair, tables)
-    fine, coarse = outer(cross, tables, part, sums)
-    return fine.reshape(COEF, 4, 4, NY), parents, coarse
+    fine, coarse_locals = outer(cross, tables, part, sums)
+    return fine.reshape(COEF, 4, 4, NY), parents, coarse_locals
 
 
 def solution(mesh):

time: 25.3 us -> 24.8 us (0.980)
  Pallas kernels: 12.3 us -> 11.5 us
  waiting for transfers between devices: 2.94 us -> 3.24 us
    pallas_call x1, Pallas kernels: 0.93 us -> 0.3 us  [pack(): pl.pallas_call(pack_kernel, in_specs=[vmem] * 5, out_specs=[vmem] * 2, ou...]
    ppermute x4, waiting for transfers between devices: 2.94 us -> 3.24 us  [exchange(): return lax.ppermute(array, axis, there + [(j, i) for i, j in there])]
    pallas_call x1 -> x2, Pallas kernels: 5.4 us -> 5.21 us  [the longest x1 3.3 us: make_tables(): pl.pallas_call(tables_kernel, in_specs=[pl.BlockSpec(memory_space=pltpu.H...]
  transfers between devices with their start and end apart: 4 -> 4, of which waited for: 2 -> 2; matrix products, arithmetic and copies ran while one was open for 0% -> 0% of each run, Pallas kernels for 37% -> 30%
where the time goes in v3:
time: 24.8 us; the launch traced here: 24.7 us
  Pallas kernels  11.5 us (46%)
  starting transfers between devices  9.24 us (37%)
  waiting for transfers between devices  3.24 us (13%)
  between operations  0.68 us (3%)
    ppermute x4, starting transfers between devices, exchange(): return lax.ppermute(array, axis, there + [(j, i) for i, j in there])  9.24 us
    pallas_call x1, Pallas kernels, inner(): pl.pallas_call(inner_kernel, in_specs=[vmem] * 4, out_specs=[vmem] * 2, o...  4.04 us
    pallas_call x1, Pallas kernels, make_tables(): pl.pallas_call(tables_kernel, in_specs=[pl.BlockSpec(memory_space=pltpu.H...  3.3 us
    ppermute x4, waiting for transfers between devices, exchange(): return lax.ppermute(array, axis, there + [(j, i) for i, j in there])  3.24 us
    pallas_call x1, Pallas kernels, outer(): pl.pallas_call(outer_kernel, in_specs=[vmem] * 4, out_specs=[vmem, vmem],...  1.95 us
    pallas_call x1, Pallas kernels, own_part(): pl.pallas_call(own_kernel, in_specs=[hbm] * 2, out_specs=[vmem] * 4, out_...  1.91 us
  transfers between devices with their start and end apart: 4, of which 2 were waited for; matrix products, arithmetic and copies ran while one was open for 0% of the time, Pallas kernels for 30%

profile of v3, /device:TPU:131, one launch (start us, length us, event | category | flops | bytes accessed | tf_op | source)
XLA Modules:
  0.0 24.7 jit_solution(1185284742137528462)
XLA Ops:
  0.6 1.9 %own_part.1 = (bf16[496,128]{1,0:T(8,128)(2,1)S(1)}, bf16[496,128]{1,0:T(8,128)(2,1)S(1)}, bf16[512,256]{1,0:T(8,128)(2,1)S(1)}, bf16[64,256]{1,0:T(8,128)(2,1)S(1)}) custom-call(bf16[784,128]{1,0:T(8,128)(2,1)} %bitcast.5, bf16[392,49]{1,0:T(8,128)(2,1)} %bitcast.6), custom_call_target="tpu_custom_call" | custom-call | tf_op jit(solution)/shard_map/own_part/pallas_call | solution.py:92
  2.5 4.2 %collective-permute-start = (bf16[496,128]{1,0:T(8,128)(2,1)S(1)}, bf16[496,128]{1,0:T(8,128)(2,1)S(1)}, u32[]{:S(2)}, u32[]{:S(2)}) collective-permute-start(bf16[496,128]{1,0:T(8,128)(2,1)S(1)} %get-tuple-element.15), channel_id=1, source_target_pairs={{8,16},{24,32},{40,48},{56,64},{72,80},{88,96},{104,112},{120,128}... | collective-permute-start | bytes 380936 | tf_op jit(solution)/shard_map/ppermute | solution.py:349
  6.7 0.4 %collective-permute-start.1 = (bf16[496,128]{1,0:T(8,128)(2,1)S(1)}, bf16[496,128]{1,0:T(8,128)(2,1)S(1)}, u32[]{:S(2)}, u32[]{:S(2)}) collective-permute-start(bf16[496,128]{1,0:T(8,128)(2,1)S(1)} %get-tuple-element.16), channel_id=1, source_target_pairs={{0,8},{16,24},{32,40},{48,56},{64,72},{80,88},{96,104},{112,120},{... | collective-permute-start | bytes 380936 | tf_op jit(solution)/shard_map/ppermute | solution.py:349
  7.1 3.3 %tables.1 = (bf16[7,3,7,128,128]{4,3,2,1,0:T(8,128)(2,1)S(1)}, bf16[49,2,2,64]{3,2,1,0:T(2,128)(2,1)}) custom-call(bf16[7,7,7,49,49]{4,3,2,1,0:T(8,128)(2,1)} %far_hbm.1, bf16[64,256]{1,0:T(8,128)(2,1)S(1)} %get-tuple-element.18.coarse_ref), custom_call_target="tpu_custom_call" | custom-call | bytes 10000000 | tf_op jit(solution)/shard_map/tables/pallas_call | solution.py:155
  10.5 1.6 %collective-permute-done.b_ref = bf16[496,128]{1,0:T(8,128)(2,1)S(1)} collective-permute-done((bf16[496,128]{1,0:T(8,128)(2,1)S(1)}, bf16[496,128]{1,0:T(8,128)(2,1)S(1)}, u32[]{:S(2)}, u32[]{:S(2)}) %collective-permute-start) | collective-permute-done | bytes 127008 | tf_op jit(solution)/shard_map/ppermute | solution.py:349
  12.0 0.0 collective-permute-done.1.a_ref
  12.0 0.3 %pack.1 = (bf16[704,256]{1,0:T(8,128)(2,1)S(1)}, bf16[704,256]{1,0:T(8,128)(2,1)S(1)}) custom-call(bf16[496,128]{1,0:T(8,128)(2,1)S(1)} %collective-permute-done.b_ref, bf16[496,128]{1,0:T(8,128)(2,1)S(1)} %collective-permute-done.1.a_ref, bf16[512,256]{1,0:T(8,128)(2,1)S(1)} %get-tuple-element.17.slabs_ref, ...), custom_call_target="tpu_custom_call" | custom-call | tf_op jit(solution)/shard_map/pack/pallas_call | solution.py:206
  12.3 1.6 %collective-permute-start.3 = (bf16[704,256]{1,0:T(8,128)(2,1)S(1)}, bf16[704,256]{1,0:T(8,128)(2,1)S(1)}, u32[]{:S(2)}, u32[]{:S(2)}) collective-permute-start(bf16[704,256]{1,0:T(8,128)(2,1)S(1)} %get-tuple-element.21.in_ref), channel_id=1, source_target_pairs={{0,1},{2,3},{4,5},{6,7},{1,0},{3,2},{5,4},{7,6},{8,9},{10,11},{12,... | collective-permute-start | bytes 1081352 | tf_op jit(solution)/shard_map/ppermute | solution.py:349
  14.0 3.0 %collective-permute-start.2 = (bf16[704,256]{1,0:T(8,128)(2,1)S(1)}, bf16[704,256]{1,0:T(8,128)(2,1)S(1)}, u32[]{:S(2)}, u32[]{:S(2)}) collective-permute-start(bf16[704,256]{1,0:T(8,128)(2,1)S(1)} %get-tuple-element.20.out_ref), channel_id=1, source_target_pairs={{1,2},{3,4},{5,6},{2,1},{4,3},{6,5},{9,10},{11,12},{13,14},{10,9},... | collective-permute-start | bytes 1081352 | tf_op jit(solution)/shard_map/ppermute | solution.py:349
  17.0 0.0 collective-permute-done.3.pair_ref
  17.0 4.0 %inner.1 = (f32[784,128]{1,0:T(8,128)S(1)}, f32[320,256]{1,0:T(8,128)S(1)}) custom-call(bf16[704,256]{1,0:T(8,128)(2,1)S(1)} %get-tuple-element.20.out_ref, bf16[704,256]{1,0:T(8,128)(2,1)S(1)} %get-tuple-element.21.in_ref, bf16[704,256]{1,0:T(8,128)(2,1)S(1)} %collective-permute-done.3.pair_ref, ...), custom_call_target="tpu_custom_call" | custom-call | flops 3000000000 | bytes 6000000 | tf_op jit(solution)/shard_map/inner/pallas_call | solution.py:290
  21.1 1.6 %collective-permute-done.2.cross_ref = bf16[704,256]{1,0:T(8,128)(2,1)S(1)} collective-permute-done((bf16[704,256]{1,0:T(8,128)(2,1)S(1)}, bf16[704,256]{1,0:T(8,128)(2,1)S(1)}, u32[]{:S(2)}, u32[]{:S(2)}) %collective-permute-start.2) | collective-permute-done | bytes 360480 | tf_op jit(solution)/shard_map/ppermute | solution.py:349
  22.7 2.0 %outer.1 = (f32[784,128]{1,0:T(8,128)}, f32[49,2,2,64]{3,2,1,0:T(2,128)}) custom-call(bf16[704,256]{1,0:T(8,128)(2,1)S(1)} %collective-permute-done.2.cross_ref, bf16[7,3,7,128,128]{4,3,2,1,0:T(8,128)(2,1)S(1)} %get-tuple-element.19.tables_ref.tables, f32[784,128]{1,0:T(8,128)S(1)} %get-tuple-element.22.part_ref, f32[320,256]{1,0:T(8,128)S(1)} %get-tuple-element.23.sums_ref), custom_call_target="tpu_custom_call" | custom-call | flops 1000000000 | bytes 5000000 | tf_op jit(solution)/shard_map/outer/pallas_call | solution.py:327
Async XLA Ops:
  2.5 9.5 %collective-permute-start = (bf16[496,128]{1,0:T(8,128)(2,1)S(1)}, bf16[496,128]{1,0:T(8,128)(2,1)S(1)}, u32[]{:S(2)}, u32[]{:S(2)}) collective-permute-start(bf16[496,128]{1,0:T(8,128)(2,1)S(1)} %get-tuple-element.15), channel_id=1, source_target_pairs={{8,16},{24,32},{40,48},{56,64},{72,80},{88,96},{104,112},{120,128}... | collective-permute-start | bytes 380936 | tf_op jit(solution)/shard_map/ppermute | solution.py:349
  6.7 5.3 %collective-permute-start.1 = (bf16[496,128]{1,0:T(8,128)(2,1)S(1)}, bf16[496,128]{1,0:T(8,128)(2,1)S(1)}, u32[]{:S(2)}, u32[]{:S(2)}) collective-permute-start(bf16[496,128]{1,0:T(8,128)(2,1)S(1)} %get-tuple-element.16), channel_id=1, source_target_pairs={{0,8},{16,24},{32,40},{48,56},{64,72},{80,88},{96,104},{112,120},{... | collective-permute-start | bytes 380936 | tf_op jit(solution)/shard_map/ppermute | solution.py:349
  12.3 4.7 %collective-permute-start.3 = (bf16[704,256]{1,0:T(8,128)(2,1)S(1)}, bf16[704,256]{1,0:T(8,128)(2,1)S(1)}, u32[]{:S(2)}, u32[]{:S(2)}) collective-permute-start(bf16[704,256]{1,0:T(8,128)(2,1)S(1)} %get-tuple-element.21.in_ref), channel_id=1, source_target_pairs={{0,1},{2,3},{4,5},{6,7},{1,0},{3,2},{5,4},{7,6},{8,9},{10,11},{12,... | collective-permute-start | bytes 1081352 | tf_op jit(solution)/shard_map/ppermute | solution.py:349
  14.0 8.7 %collective-permute-start.2 = (bf16[704,256]{1,0:T(8,128)(2,1)S(1)}, bf16[704,256]{1,0:T(8,128)(2,1)S(1)}, u32[]{:S(2)}, u32[]{:S(2)}) collective-permute-start(bf16[704,256]{1,0:T(8,128)(2,1)S(1)} %get-tuple-element.20.out_ref), channel_id=1, source_target_pairs={{1,2},{3,4},{5,6},{2,1},{4,3},{6,5},{9,10},{11,12},{13,14},{10,9},... | collective-permute-start | bytes 1081352 | tf_op jit(solution)/shard_map/ppermute | solution.py:349

commit v4 on v3

--- a/solution.py
+++ b/solution.py
@@ -12,10 +12,11 @@
 SLOT = 64
 NY = 128
 HY = 64
-FINE = 4 * NY
-ROWS = FINE + 3 * HY
-NEAR = 8 * COEF
-SIDE = 496
+BLOCK = 208
+PAIR = 112
+SIDE = 2 * BLOCK + PAIR
+COLUMN = 4 * BLOCK
+ROWS = COLUMN + 3 * PAIR
 SEG = NY + 8
 VMEM = 20 * 2**20
 
@@ -46,8 +47,8 @@
 
 
 def own_kernel(
-    own_hbm, up_hbm, a_ref, b_ref, slabs_ref, coarse_ref,
-    own, up, brick, packed, wide, pairs, halves, message, sems,
+    own_hbm, up_hbm, a_ref, b_ref, packed_ref, coarse_ref,
+    own, up, brick, packed, wide, pairs, halves, parents_t, sems,
 ):
     odd = lax.rem(lax.axis_index("wide"), 2)
     get_up = pltpu.make_async_copy(up_hbm, up, sems.at[0])
@@ -66,24 +67,24 @@
     get_own.wait()
     brick[pl.ds(0, 16 * COEF), :] = own[...].astype(F32)
     cells = [brick[pl.ds(cell, SLOT, stride=16), :] for cell in range(16)]
-    for cell in range(16):
-        packed[pl.ds(COEF * cell, SLOT), :] = cells[cell]
     order = [(2 * px + cx) * 4 + 2 * zp + cz for px in range(2) for zp in range(2) for cx in range(2) for cz in range(2)]
+    for at, cell in enumerate(order):
+        packed[pl.ds(BLOCK * (at // 4) + COEF * (at % 4), SLOT), :] = cells[cell]
     turned = turn(unit, jnp.concatenate([cells[cell] for cell in order], axis=0)).astype(BF16)
-    parts = [turned[:, 256 * at : 256 * at + 256] for at in range(4)]
-    sums = dot(jnp.concatenate(parts, axis=0), pairs[...])
+    packed_ref[...] = packed[pl.ds(0, COLUMN), :].astype(BF16)
+    a_ref[pl.ds(0, 2 * BLOCK), :] = packed_ref[pl.ds(pl.multiple_of((1 - odd) * 2 * BLOCK, 16), 2 * BLOCK), :]
+    b_ref[pl.ds(0, 2 * BLOCK), :] = packed_ref[pl.ds(pl.multiple_of(odd * 2 * BLOCK, 16), 2 * BLOCK), :]
+    sums = dot(jnp.concatenate([turned[:, 256 * at : 256 * at + 256] for at in range(4)], axis=0), pairs[...])
     for at in range(4):
-        slabs_ref[pl.ds(at * NY, NY), :] = parts[at]
         halves[at] = sums[at * NY : at * NY + NY]
     parents = [to_parents(halves, 2 * px, low) for px in range(2)]
-    for px in range(2):
-        coarse_ref[:, pl.ds(128 * px, 128)] = parents[px]
-    turned = turn(unit, jnp.concatenate(parents, axis=0))
-    message[pl.ds(NEAR, SLOT), :] = turned[0:SLOT]
-    message[pl.ds(NEAR + COEF, SLOT), :] = turned[SLOT:128]
-    for ref, half in ((b_ref, odd), (a_ref, 1 - odd)):
-        message[pl.ds(0, NEAR), :] = packed[pl.ds(pl.multiple_of(half * NEAR, 8), NEAR), :]
-        ref[...] = message[pl.ds(0, SIDE), :].astype(BF16)
+    coarse = jnp.concatenate(parents, axis=0)
+    coarse_ref[...] = coarse
+    turned = turn(unit, coarse)
+    parents_t[pl.ds(0, SLOT), :] = turned[0:SLOT]
+    parents_t[pl.ds(COEF, SLOT), :] = turned[SLOT:128]
+    for ref in (a_ref, b_ref):
+        ref[pl.ds(2 * BLOCK, PAIR), :] = parents_t[pl.ds(0, PAIR), :].astype(BF16)
 
 
 def own_part(own, up):
@@ -96,18 +97,18 @@
         out_shape=[
             pltpu.VMEM((SIDE, NY), BF16),
             pltpu.VMEM((SIDE, NY), BF16),
-            pltpu.VMEM((FINE, 256), BF16),
-            pltpu.VMEM((HY, 256), BF16),
+            pltpu.VMEM((COLUMN, NY), BF16),
+            pltpu.VMEM((128, 128), BF16),
         ],
         scratch_shapes=[
             pltpu.VMEM((16 * COEF, NY), BF16),
             pltpu.VMEM((8 * COEF, COEF), BF16),
             pltpu.VMEM((16 * SLOT, NY), F32),
-            pltpu.VMEM((16 * COEF + 16, NY), F32),
+            pltpu.VMEM((COLUMN + 16, NY), F32),
             pltpu.VMEM((8 * COEF, COEF), F32),
             pltpu.VMEM((256, 128), BF16),
             pltpu.VMEM((4, NY, 128), F32),
-            pltpu.VMEM((SIDE + 16, NY), F32),
+            pltpu.VMEM((120, NY), F32),
             pltpu.SemaphoreType.DMA((2,)),
         ],
         compiler_params=pltpu.CompilerParams(vmem_limit_bytes=VMEM),
@@ -122,8 +123,7 @@
     for dx in range(7):
         fetch(dx).start()
 
-    cells = jnp.concatenate([coarse_ref[:, pl.ds(128 * px, 128)] for px in range(2)], axis=0)
-    turned = turn(eye(NY), cells)
+    turned = turn(eye(NY), coarse_ref[...])
     for px in range(2):
         for z in range(2):
             block = turned[z * SLOT : z * SLOT + COEF, px * HY : (px + 1) * HY]
@@ -171,47 +171,31 @@
     )(pltpu.with_memory_space_constraint(far, pltpu.HBM), pltpu.with_memory_space_constraint(coarse, pltpu.VMEM))
 
 
-def pack_kernel(b_ref, a_ref, slabs_ref, coarse_ref, tables_ref, out_ref, in_ref, bricks):
+def pack_kernel(b_ref, a_ref, packed_ref, mine_ref, tables_ref, out_ref, in_ref):
     odd, core = lax.rem(lax.axis_index("wide"), 2), core_parity()
-    unit = eye(NY)
-    refs = (out_ref, in_ref)
-    for q in range(2):
+    for q, ref in enumerate((out_ref, in_ref)):
+        zp = q + core - 2 * q * core
         for px in range(2):
-            row = pl.multiple_of((2 * px + q + core - 2 * q * core) * NY, NY)
-            refs[q][pl.ds((1 + px) * NY, NY), :] = slabs_ref[pl.ds(row, NY), :]
-        refs[q][pl.ds(FINE + HY, HY), :] = coarse_ref[...]
-    for at, (side, above) in enumerate(((b_ref, odd), (a_ref, 1 - odd))):
-        brick = bricks.at[at]
-        brick[pl.ds(0, SIDE), :] = side[...].astype(F32)
-        brick[pl.ds(SIDE, 16), :] = jnp.zeros((16, NY), F32)
-        for q in range(2):
-            zp = q + core - 2 * q * core
-            cells = []
-            for cx in range(2):
-                for cz in range(2):
-                    here = [brick[pl.ds(COEF * (4 * cx + 2 * z + cz), SLOT), :] for z in range(2)]
-                    cells.append(jnp.where(zp == 0, here[0], here[1]))
-            turned = turn(unit, jnp.concatenate(cells, axis=0)).astype(BF16)
-            refs[q][pl.ds(pl.multiple_of(above * 3 * NY, NY), NY), :] = turned
-        cells = jnp.concatenate([brick[pl.ds(NEAR + COEF * z, SLOT), :] for z in range(2)], axis=0)
-        turned = turn(unit, cells).astype(BF16)
-        for ref in refs:
-            row = pl.multiple_of(FINE + above * 2 * HY, HY)
-            for px in range(2):
-                ref[pl.ds(row, HY), pl.ds(128 * px, 128)] = turned[px * HY : (px + 1) * HY]
-
-
-def pack(b, a, slabs, coarse, tables):
+            row = pl.multiple_of((2 * px + zp) * BLOCK, 16)
+            ref[pl.ds((1 + px) * BLOCK, BLOCK), :] = packed_ref[pl.ds(row, BLOCK), :]
+        ref[pl.ds(COLUMN + PAIR, PAIR), :] = mine_ref[pl.ds(2 * BLOCK, PAIR), :]
+        for side, above in ((b_ref, odd), (a_ref, 1 - odd)):
+            row = pl.multiple_of(above * 3 * BLOCK, 16)
+            ref[pl.ds(row, BLOCK), :] = side[pl.ds(pl.multiple_of(zp * BLOCK, 16), BLOCK), :]
+            row = pl.multiple_of(COLUMN + above * 2 * PAIR, 16)
+            ref[pl.ds(row, PAIR), :] = side[pl.ds(2 * BLOCK, PAIR), :]
+
+
+def pack(b, a, packed, mine, tables):
     vmem = pl.BlockSpec(memory_space=pltpu.VMEM)
     return pl.pallas_call(
         pack_kernel,
         in_specs=[vmem] * 5,
         out_specs=[vmem] * 2,
-        out_shape=[jax.ShapeDtypeStruct((ROWS, 256), BF16)] * 2,
-        scratch_shapes=[pltpu.VMEM((2, SIDE + 16, NY), F32)],
+        out_shape=[jax.ShapeDtypeStruct((ROWS, NY), BF16)] * 2,
         compiler_params=pltpu.CompilerParams(vmem_limit_bytes=VMEM),
         name="pack",
-    )(b, a, *[pltpu.with_memory_space_constraint(x, pltpu.VMEM) for x in (slabs, coarse, tables)])
+    )(b, a, *[pltpu.with_memory_space_constraint(x, pltpu.VMEM) for x in (packed, mine, tables)])
 
 
 def operator(tables, dy, at, skip=False):
@@ -222,13 +206,15 @@
     )
 
 
-def slabs(ref):
-    part = [ref[pl.ds(x * NY, NY), :] for x in range(4)]
-    return jnp.concatenate([jnp.concatenate(part[x : x + 3], axis=1) for x in range(2)], axis=0)
-
-
-def coarse_slab(ref):
-    return jnp.concatenate([ref[pl.ds(FINE + x * HY, HY), :] for x in range(3)], axis=1)
+def sources_of(ref, rows):
+    rows[pl.ds(0, ROWS), :] = ref[...].astype(F32)
+    rows[pl.ds(ROWS, 16), :] = jnp.zeros((16, NY), F32)
+    cells = [rows[pl.ds(BLOCK * at + COEF * cell, SLOT), :] for at in range(4) for cell in range(4)]
+    cells += [rows[pl.ds(COLUMN + PAIR * at + COEF * z, SLOT), :] for at in range(3) for z in range(2)]
+    turned = turn(eye(NY), jnp.concatenate(cells, axis=0)).astype(BF16)
+    fine = jnp.concatenate([turned[:, 0:768], turned[:, 256:1024]], axis=0)
+    parts = [turned[px * HY : (px + 1) * HY, 1024 + 128 * at : 1152 + 128 * at] for at in range(3) for px in range(2)]
+    return fine, jnp.concatenate(parts, axis=1)
 
 
 def clear_gaps(spread, count):
@@ -262,12 +248,18 @@
         fine_ref[pl.ds(first, COEF, stride=16), :] = done[child * SLOT : child * SLOT + COEF]
 
 
-def inner_kernel(out_ref, in_ref, pair_ref, tables, part_ref, sums_ref, sources, beyond, spread):
+def inner_kernel(out_ref, in_ref, pair_ref, tables, part_ref, sums_ref, sources, beyond, spread, rows):
     core = core_parity()
     sign = 1 - 2 * core
     clear_gaps(spread, 4)
-    sources[...] = jnp.concatenate([slabs(out_ref), slabs(in_ref), coarse_slab(out_ref)], axis=0)
-    beyond[...] = jnp.concatenate([slabs(pair_ref), coarse_slab(pair_ref)], axis=0)
+    for at, ref in enumerate((out_ref, in_ref, pair_ref)):
+        fine, coarse = sources_of(ref, rows.at[at])
+        if at < 2:
+            sources[pl.ds(256 * at, 256), :] = fine
+            sources[pl.ds(512, HY), :] = coarse
+        else:
+            beyond[pl.ds(0, 256), :] = fine
+            beyond[pl.ds(256, HY), :] = coarse
     for dy in range(7):
         if 2 <= dy <= 4:
             beside = jnp.concatenate([sources[:, 0:256], sources[:, 512:768]], axis=1)
@@ -296,9 +288,10 @@
             jax.ShapeDtypeStruct((2 * NY + HY, 256), F32),
         ],
         scratch_shapes=[
-            pltpu.VMEM((FINE + HY, 768), BF16),
+            pltpu.VMEM((4 * NY + HY, 768), BF16),
             pltpu.VMEM((2 * NY + HY, 768), BF16),
             pltpu.VMEM((7, 4 * SEG + HY + 16, 256), F32),
+            pltpu.VMEM((3, ROWS + 16, NY), F32),
         ],
         compiler_params=pltpu.CompilerParams(vmem_limit_bytes=VMEM),
         cost_estimate=pl.CostEstimate(flops=3_000_000_000, bytes_accessed=6_000_000, transcendentals=0),
@@ -306,10 +299,10 @@
     )(out, into, pair, pltpu.with_memory_space_constraint(tables, pltpu.VMEM))
 
 
-def outer_kernel(cross_ref, tables, part_ref, sums_ref, fine_ref, coarse_ref, sources, spread, shuffled):
+def outer_kernel(cross_ref, tables, part_ref, sums_ref, fine_ref, coarse_ref, sources, spread, shuffled, rows):
     core = core_parity()
     clear_gaps(spread, 2)
-    sources[...] = jnp.concatenate([slabs(cross_ref), coarse_slab(cross_ref)], axis=0)
+    sources[...] = jnp.concatenate(sources_of(cross_ref, rows), axis=0)
     for dy in range(7):
         found = dot(sources[...], operator(tables, dy, 2 * core))
         put(spread.at[dy], found[0:256], found[256:])
@@ -336,6 +329,7 @@
             pltpu.VMEM((2 * NY + HY, 768), BF16),
             pltpu.VMEM((7, 2 * SEG + HY + 16, 256), F32),
             pltpu.VMEM((4 * COEF, HY), F32),
+            pltpu.VMEM((ROWS + 16, NY), F32),
         ],
         compiler_params=pltpu.CompilerParams(vmem_limit_bytes=VMEM),
         cost_estimate=pl.CostEstimate(flops=1_000_000_000, bytes_accessed=5_000_000, transcendentals=0),
@@ -351,11 +345,11 @@
 
 def shards(multipoles, translate_far, translate_up):
     up = translate_up.transpose(1, 0, 2).reshape(8 * COEF, COEF)
-    to_a, to_b, slabs, coarse = own_part(multipoles.reshape(16 * COEF, NY), up)
+    to_a, to_b, packed, coarse = own_part(multipoles.reshape(16 * COEF, NY), up)
     b = exchange(to_b, "wide", 1)
     a = exchange(to_a, "wide", 0)
     tables, parents = make_tables(translate_far, coarse)
-    out, into = pack(b, a, slabs, coarse, tables)
+    out, into = pack(b, a, packed, to_b, tables)
     pair = exchange(into, "narrow", 0)
     cross = exchange(out, "narrow", 1)
     part, sums = inner(out, into, pair, tables)

time: 24.8 us -> 24.2 us (0.976)
  waiting for transfers between devices: 3.24 us -> 2.43 us
    ppermute x4, waiting for transfers between devices: 3.24 us -> 2.43 us  [exchange(): return lax.ppermute(array, axis, there + [(j, i) for i, j in there])]
    pallas_call x1, Pallas kernels: 4.04 us -> 4.37 us  [inner(): pl.pallas_call(inner_kernel, in_specs=[vmem] * 4, out_specs=[vmem] * 2, o...]
  transfers between devices with their start and end apart: 4 -> 4, of which waited for: 2 -> 2; matrix products, arithmetic and copies ran while one was open for 0% -> 0% of each run, Pallas kernels for 30% -> 32%
where the time goes in v4:
time: 24.2 us; the launch traced here: 24.1 us
  Pallas kernels  11.7 us (48%)
  starting transfers between devices  9.24 us (38%)
  waiting for transfers between devices  2.43 us (10%)
  between operations  0.69 us (3%)
    ppermute x4, starting transfers between devices, exchange(): return lax.ppermute(array, axis, there + [(j, i) for i, j in there])  9.24 us
    pallas_call x1, Pallas kernels, inner(): pl.pallas_call(inner_kernel, in_specs=[vmem] * 4, out_specs=[vmem] * 2, o...  4.37 us
    pallas_call x1, Pallas kernels, make_tables(): pl.pallas_call(tables_kernel, in_specs=[pl.BlockSpec(memory_space=pltpu.H...  3.3 us
    ppermute x4, waiting for transfers between devices, exchange(): return lax.ppermute(array, axis, there + [(j, i) for i, j in there])  2.43 us
    pallas_call x1, Pallas kernels, outer(): pl.pallas_call(outer_kernel, in_specs=[vmem] * 4, out_specs=[vmem, vmem],...  2.11 us
    pallas_call x1, Pallas kernels, own_part(): pl.pallas_call(own_kernel, in_specs=[hbm] * 2, out_specs=[vmem] * 4, out_...  1.9 us
  transfers between devices with their start and end apart: 4, of which 2 were waited for; matrix products, arithmetic and copies ran while one was open for 0% of the time, Pallas kernels for 32%

profile of v4, /device:TPU:131, one launch (start us, length us, event | category | flops | bytes accessed | tf_op | source)
XLA Modules:
  0.0 24.1 jit_solution(4575796316446263767)
XLA Ops:
  0.6 1.9 %own_part.1 = (bf16[528,128]{1,0:T(8,128)(2,1)S(1)}, bf16[528,128]{1,0:T(8,128)(2,1)S(1)}, bf16[832,128]{1,0:T(8,128)(2,1)S(1)}, bf16[128,128]{1,0:T(8,128)(2,1)S(1)}) custom-call(bf16[784,128]{1,0:T(8,128)(2,1)} %bitcast.5, bf16[392,49]{1,0:T(8,128)(2,1)} %bitcast.6), custom_call_target="tpu_custom_call" | custom-call | tf_op jit(solution)/shard_map/own_part/pallas_call | solution.py:93
  2.5 4.2 %collective-permute-start = (bf16[528,128]{1,0:T(8,128)(2,1)S(1)}, bf16[528,128]{1,0:T(8,128)(2,1)S(1)}, u32[]{:S(2)}, u32[]{:S(2)}) collective-permute-start(bf16[528,128]{1,0:T(8,128)(2,1)S(1)} %get-tuple-element.15.mine_ref), channel_id=1, source_target_pairs={{8,16},{24,32},{40,48},{56,64},{72,80},{88,96},{104,112},{120,128}... | collective-permute-start | bytes 405512 | tf_op jit(solution)/shard_map/ppermute | solution.py:343
  6.7 0.4 %collective-permute-start.1 = (bf16[528,128]{1,0:T(8,128)(2,1)S(1)}, bf16[528,128]{1,0:T(8,128)(2,1)S(1)}, u32[]{:S(2)}, u32[]{:S(2)}) collective-permute-start(bf16[528,128]{1,0:T(8,128)(2,1)S(1)} %get-tuple-element.16), channel_id=1, source_target_pairs={{0,8},{16,24},{32,40},{48,56},{64,72},{80,88},{96,104},{112,120},{... | collective-permute-start | bytes 405512 | tf_op jit(solution)/shard_map/ppermute | solution.py:343
  7.1 3.3 %tables.1 = (bf16[7,3,7,128,128]{4,3,2,1,0:T(8,128)(2,1)S(1)}, bf16[49,2,2,64]{3,2,1,0:T(2,128)(2,1)}) custom-call(bf16[7,7,7,49,49]{4,3,2,1,0:T(8,128)(2,1)} %far_hbm.1, bf16[128,128]{1,0:T(8,128)(2,1)S(1)} %get-tuple-element.18.coarse_ref), custom_call_target="tpu_custom_call" | custom-call | bytes 10000000 | tf_op jit(solution)/shard_map/tables/pallas_call | solution.py:155
  10.4 1.8 %collective-permute-done.b_ref = bf16[528,128]{1,0:T(8,128)(2,1)S(1)} collective-permute-done((bf16[528,128]{1,0:T(8,128)(2,1)S(1)}, bf16[528,128]{1,0:T(8,128)(2,1)S(1)}, u32[]{:S(2)}, u32[]{:S(2)}) %collective-permute-start) | collective-permute-done | bytes 135200 | tf_op jit(solution)/shard_map/ppermute | solution.py:343
  12.2 0.0 collective-permute-done.1.a_ref
  12.2 0.1 pack.1
  12.3 1.6 %collective-permute-start.3 = (bf16[1168,128]{1,0:T(8,128)(2,1)S(1)}, bf16[1168,128]{1,0:T(8,128)(2,1)S(1)}, u32[]{:S(2)}, u32[]{:S(2)}) collective-permute-start(bf16[1168,128]{1,0:T(8,128)(2,1)S(1)} %get-tuple-element.21.in_ref), channel_id=1, source_target_pairs={{0,1},{2,3},{4,5},{6,7},{1,0},{3,2},{5,4},{7,6},{8,9},{10,11},{12,... | collective-permute-start | bytes 897032 | tf_op jit(solution)/shard_map/ppermute | solution.py:343
  13.9 3.0 %collective-permute-start.2 = (bf16[1168,128]{1,0:T(8,128)(2,1)S(1)}, bf16[1168,128]{1,0:T(8,128)(2,1)S(1)}, u32[]{:S(2)}, u32[]{:S(2)}) collective-permute-start(bf16[1168,128]{1,0:T(8,128)(2,1)S(1)} %get-tuple-element.20.out_ref), channel_id=1, source_target_pairs={{1,2},{3,4},{5,6},{2,1},{4,3},{6,5},{9,10},{11,12},{13,14},{10,9},... | collective-permute-start | bytes 897032 | tf_op jit(solution)/shard_map/ppermute | solution.py:343
  16.9 0.0 collective-permute-done.3.pair_ref
  16.9 4.4 %inner.1 = (f32[784,128]{1,0:T(8,128)S(1)}, f32[320,256]{1,0:T(8,128)S(1)}) custom-call(bf16[1168,128]{1,0:T(8,128)(2,1)S(1)} %get-tuple-element.20.out_ref, bf16[1168,128]{1,0:T(8,128)(2,1)S(1)} %get-tuple-element.21.in_ref, bf16[1168,128]{1,0:T(8,128)(2,1)S(1)} %collective-permute-done.3.pair_ref, ...), custom_call_target="tpu_custom_call" | custom-call | flops 3000000000 | bytes 6000000 | tf_op jit(solution)/shard_map/inner/pallas_call | solution.py:282
  21.3 0.7 %collective-permute-done.2.cross_ref = bf16[1168,128]{1,0:T(8,128)(2,1)S(1)} collective-permute-done((bf16[1168,128]{1,0:T(8,128)(2,1)S(1)}, bf16[1168,128]{1,0:T(8,128)(2,1)S(1)}, u32[]{:S(2)}, u32[]{:S(2)}) %collective-permute-start.2) | collective-permute-done | bytes 299040 | tf_op jit(solution)/shard_map/ppermute | solution.py:343
  22.0 2.1 %outer.1 = (f32[784,128]{1,0:T(8,128)}, f32[49,2,2,64]{3,2,1,0:T(2,128)}) custom-call(bf16[1168,128]{1,0:T(8,128)(2,1)S(1)} %collective-permute-done.2.cross_ref, bf16[7,3,7,128,128]{4,3,2,1,0:T(8,128)(2,1)S(1)} %get-tuple-element.19.tables_ref.tables, f32[784,128]{1,0:T(8,128)S(1)} %get-tuple-element.22.part_ref, f32[320,256]{1,0:T(8,128)S(1)} %get-tuple-element.23.sums_ref), custom_call_target="tpu_custom_call" | custom-call | flops 1000000000 | bytes 5000000 | tf_op jit(solution)/shard_map/outer/pallas_call | solution.py:320
Async XLA Ops:
  2.5 9.7 %collective-permute-start = (bf16[528,128]{1,0:T(8,128)(2,1)S(1)}, bf16[528,128]{1,0:T(8,128)(2,1)S(1)}, u32[]{:S(2)}, u32[]{:S(2)}) collective-permute-start(bf16[528,128]{1,0:T(8,128)(2,1)S(1)} %get-tuple-element.15.mine_ref), channel_id=1, source_target_pairs={{8,16},{24,32},{40,48},{56,64},{72,80},{88,96},{104,112},{120,128}... | collective-permute-start | bytes 405512 | tf_op jit(solution)/shard_map/ppermute | solution.py:343
  6.7 5.5 %collective-permute-start.1 = (bf16[528,128]{1,0:T(8,128)(2,1)S(1)}, bf16[528,128]{1,0:T(8,128)(2,1)S(1)}, u32[]{:S(2)}, u32[]{:S(2)}) collective-permute-start(bf16[528,128]{1,0:T(8,128)(2,1)S(1)} %get-tuple-element.16), channel_id=1, source_target_pairs={{0,8},{16,24},{32,40},{48,56},{64,72},{80,88},{96,104},{112,120},{... | collective-permute-start | bytes 405512 | tf_op jit(solution)/shard_map/ppermute | solution.py:343
  12.3 4.7 %collective-permute-start.3 = (bf16[1168,128]{1,0:T(8,128)(2,1)S(1)}, bf16[1168,128]{1,0:T(8,128)(2,1)S(1)}, u32[]{:S(2)}, u32[]{:S(2)}) collective-permute-start(bf16[1168,128]{1,0:T(8,128)(2,1)S(1)} %get-tuple-element.21.in_ref), channel_id=1, source_target_pairs={{0,1},{2,3},{4,5},{6,7},{1,0},{3,2},{5,4},{7,6},{8,9},{10,11},{12,... | collective-permute-start | bytes 897032 | tf_op jit(solution)/shard_map/ppermute | solution.py:343
  13.9 8.1 %collective-permute-start.2 = (bf16[1168,128]{1,0:T(8,128)(2,1)S(1)}, bf16[1168,128]{1,0:T(8,128)(2,1)S(1)}, u32[]{:S(2)}, u32[]{:S(2)}) collective-permute-start(bf16[1168,128]{1,0:T(8,128)(2,1)S(1)} %get-tuple-element.20.out_ref), channel_id=1, source_target_pairs={{1,2},{3,4},{5,6},{2,1},{4,3},{6,5},{9,10},{11,12},{13,14},{10,9},... | collective-permute-start | bytes 897032 | tf_op jit(solution)/shard_map/ppermute | solution.py:343

commit v5 on v4

--- a/solution.py
+++ b/solution.py
@@ -39,16 +39,9 @@
     return lax.dot_general(unit, cells.astype(BF16), NT, preferred_element_type=F32)
 
 
-def to_parents(halves, at, low):
-    z0, z1 = halves.at[at], halves.at[at + 1]
-    first = z0[pl.ds(0, HY, stride=2), :] + pltpu.roll(z0[pl.ds(1, HY, stride=2), :], SLOT, 1)
-    second = pltpu.roll(z1[pl.ds(0, HY, stride=2), :], SLOT, 1) + z1[pl.ds(1, HY, stride=2), :]
-    return jnp.where(low, first, second).astype(BF16)
-
-
 def own_kernel(
     own_hbm, up_hbm, a_ref, b_ref, packed_ref, coarse_ref,
-    own, up, brick, packed, wide, pairs, halves, parents_t, sems,
+    own, up, brick, packed, wide, pairs, parents_t, sems,
 ):
     odd = lax.rem(lax.axis_index("wide"), 2)
     get_up = pltpu.make_async_copy(up_hbm, up, sems.at[0])
@@ -57,32 +50,34 @@
     get_up.start()
     pairs[...] = jnp.zeros_like(pairs)
     brick[pl.ds(16 * COEF, 16 * (SLOT - COEF)), :] = jnp.zeros((16 * (SLOT - COEF), NY), F32)
-    unit = eye(NY)
-    low = lax.broadcasted_iota(jnp.int32, (HY, 128), 1) < SLOT
     get_up.wait()
     wide[...] = up[...].astype(F32)
     for child in range(8):
         block = wide[pl.ds(child, COEF, stride=8), :].astype(BF16)
         pairs[pl.ds(SLOT * (child // 2), COEF), pl.ds(SLOT * (child % 2), COEF)] = block
+    pairs_t = pairs[...].T
     get_own.wait()
     brick[pl.ds(0, 16 * COEF), :] = own[...].astype(F32)
     cells = [brick[pl.ds(cell, SLOT, stride=16), :] for cell in range(16)]
     order = [(2 * px + cx) * 4 + 2 * zp + cz for px in range(2) for zp in range(2) for cx in range(2) for cz in range(2)]
     for at, cell in enumerate(order):
         packed[pl.ds(BLOCK * (at // 4) + COEF * (at % 4), SLOT), :] = cells[cell]
-    turned = turn(unit, jnp.concatenate([cells[cell] for cell in order], axis=0)).astype(BF16)
     packed_ref[...] = packed[pl.ds(0, COLUMN), :].astype(BF16)
     a_ref[pl.ds(0, 2 * BLOCK), :] = packed_ref[pl.ds(pl.multiple_of((1 - odd) * 2 * BLOCK, 16), 2 * BLOCK), :]
     b_ref[pl.ds(0, 2 * BLOCK), :] = packed_ref[pl.ds(pl.multiple_of(odd * 2 * BLOCK, 16), 2 * BLOCK), :]
-    sums = dot(jnp.concatenate([turned[:, 256 * at : 256 * at + 256] for at in range(4)], axis=0), pairs[...])
-    for at in range(4):
-        halves[at] = sums[at * NY : at * NY + NY]
-    parents = [to_parents(halves, 2 * px, low) for px in range(2)]
-    coarse = jnp.concatenate(parents, axis=0)
-    coarse_ref[...] = coarse
-    turned = turn(unit, coarse)
-    parents_t[pl.ds(0, SLOT), :] = turned[0:SLOT]
-    parents_t[pl.ds(COEF, SLOT), :] = turned[SLOT:128]
+    lane = lax.broadcasted_iota(jnp.int32, (SLOT, NY), 1)
+    even = 2 * lax.rem(lane, HY)
+    for zp in range(2):
+        found = []
+        for px in range(2):
+            part = jnp.concatenate([cells[cell] for cell in order[8 * px + 4 * zp : 8 * px + 4 * zp + 4]], axis=0)
+            both = dot(pairs_t, part.astype(BF16))
+            first = jnp.take_along_axis(both[0:SLOT], even, axis=1, mode="promise_in_bounds")
+            second = jnp.take_along_axis(both[SLOT:128], even + 1, axis=1, mode="promise_in_bounds")
+            found.append(first + second)
+        parents = jnp.where(lane < HY, found[0], found[1])
+        parents_t[pl.ds(COEF * zp, SLOT), :] = parents
+        coarse_ref[pl.ds(SLOT * zp, SLOT), :] = parents.astype(BF16)
     for ref in (a_ref, b_ref):
         ref[pl.ds(2 * BLOCK, PAIR), :] = parents_t[pl.ds(0, PAIR), :].astype(BF16)
 
@@ -107,7 +102,6 @@
             pltpu.VMEM((COLUMN + 16, NY), F32),
             pltpu.VMEM((8 * COEF, COEF), F32),
             pltpu.VMEM((256, 128), BF16),
-            pltpu.VMEM((4, NY, 128), F32),
             pltpu.VMEM((120, NY), F32),
             pltpu.SemaphoreType.DMA((2,)),
         ],
@@ -123,7 +117,7 @@
     for dx in range(7):
         fetch(dx).start()
 
-    turned = turn(eye(NY), coarse_ref[...])
+    turned = coarse_ref[...].astype(F32)
     for px in range(2):
         for z in range(2):
             block = turned[z * SLOT : z * SLOT + COEF, px * HY : (px + 1) * HY]

time: 24.2 us -> 24 us (level)
  no operation moved by 1% of the time
where the time goes in v5:
time: 24 us; the launch traced here: 23.9 us
  Pallas kernels  11.5 us (48%)
  starting transfers between devices  9.24 us (38%)
  waiting for transfers between devices  2.43 us (10%)
  between operations  0.69 us (3%)
    ppermute x4, starting transfers between devices, exchange(): return lax.ppermute(array, axis, there + [(j, i) for i, j in there])  9.24 us
    pallas_call x1, Pallas kernels, inner(): pl.pallas_call(inner_kernel, in_specs=[vmem] * 4, out_specs=[vmem] * 2, o...  4.37 us
    pallas_call x1, Pallas kernels, make_tables(): pl.pallas_call(tables_kernel, in_specs=[pl.BlockSpec(memory_space=pltpu.H...  3.3 us
    ppermute x4, waiting for transfers between devices, exchange(): return lax.ppermute(array, axis, there + [(j, i) for i, j in there])  2.43 us
    pallas_call x1, Pallas kernels, outer(): pl.pallas_call(outer_kernel, in_specs=[vmem] * 4, out_specs=[vmem, vmem],...  2.1 us
    pallas_call x1, Pallas kernels, own_part(): pl.pallas_call(own_kernel, in_specs=[hbm] * 2, out_specs=[vmem] * 4, out_...  1.71 us
  transfers between devices with their start and end apart: 4, of which 2 were waited for; matrix products, arithmetic and copies ran while one was open for 0% of the time, Pallas kernels for 32%

profile of v5, /device:TPU:131, one launch (start us, length us, event | category | flops | bytes accessed | tf_op | source)
XLA Modules:
  0.0 23.9 jit_solution(8993102009283499949)
XLA Ops:
  0.6 1.7 %own_part.1 = (bf16[528,128]{1,0:T(8,128)(2,1)S(1)}, bf16[528,128]{1,0:T(8,128)(2,1)S(1)}, bf16[832,128]{1,0:T(8,128)(2,1)S(1)}, bf16[128,128]{1,0:T(8,128)(2,1)S(1)}) custom-call(bf16[784,128]{1,0:T(8,128)(2,1)} %bitcast.5, bf16[392,49]{1,0:T(8,128)(2,1)} %bitcast.6), custom_call_target="tpu_custom_call" | custom-call | tf_op jit(solution)/shard_map/own_part/pallas_call | solution.py:88
  2.3 4.2 %collective-permute-start = (bf16[528,128]{1,0:T(8,128)(2,1)S(1)}, bf16[528,128]{1,0:T(8,128)(2,1)S(1)}, u32[]{:S(2)}, u32[]{:S(2)}) collective-permute-start(bf16[528,128]{1,0:T(8,128)(2,1)S(1)} %get-tuple-element.15.mine_ref), channel_id=1, source_target_pairs={{8,16},{24,32},{40,48},{56,64},{72,80},{88,96},{104,112},{120,128}... | collective-permute-start | bytes 405512 | tf_op jit(solution)/shard_map/ppermute | solution.py:337
  6.5 0.4 %collective-permute-start.1 = (bf16[528,128]{1,0:T(8,128)(2,1)S(1)}, bf16[528,128]{1,0:T(8,128)(2,1)S(1)}, u32[]{:S(2)}, u32[]{:S(2)}) collective-permute-start(bf16[528,128]{1,0:T(8,128)(2,1)S(1)} %get-tuple-element.16), channel_id=1, source_target_pairs={{0,8},{16,24},{32,40},{48,56},{64,72},{80,88},{96,104},{112,120},{... | collective-permute-start | bytes 405512 | tf_op jit(solution)/shard_map/ppermute | solution.py:337
  6.9 3.3 %tables.1 = (bf16[7,3,7,128,128]{4,3,2,1,0:T(8,128)(2,1)S(1)}, bf16[49,2,2,64]{3,2,1,0:T(2,128)(2,1)}) custom-call(bf16[7,7,7,49,49]{4,3,2,1,0:T(8,128)(2,1)} %far_hbm.1, bf16[128,128]{1,0:T(8,128)(2,1)S(1)} %get-tuple-element.18.coarse_ref), custom_call_target="tpu_custom_call" | custom-call | bytes 10000000 | tf_op jit(solution)/shard_map/tables/pallas_call | solution.py:149
  10.2 1.8 %collective-permute-done.b_ref = bf16[528,128]{1,0:T(8,128)(2,1)S(1)} collective-permute-done((bf16[528,128]{1,0:T(8,128)(2,1)S(1)}, bf16[528,128]{1,0:T(8,128)(2,1)S(1)}, u32[]{:S(2)}, u32[]{:S(2)}) %collective-permute-start) | collective-permute-done | bytes 135200 | tf_op jit(solution)/shard_map/ppermute | solution.py:337
  12.0 0.0 collective-permute-done.1.a_ref
  12.0 0.1 pack.1
  12.1 1.6 %collective-permute-start.3 = (bf16[1168,128]{1,0:T(8,128)(2,1)S(1)}, bf16[1168,128]{1,0:T(8,128)(2,1)S(1)}, u32[]{:S(2)}, u32[]{:S(2)}) collective-permute-start(bf16[1168,128]{1,0:T(8,128)(2,1)S(1)} %get-tuple-element.21.in_ref), channel_id=1, source_target_pairs={{0,1},{2,3},{4,5},{6,7},{1,0},{3,2},{5,4},{7,6},{8,9},{10,11},{12,... | collective-permute-start | bytes 897032 | tf_op jit(solution)/shard_map/ppermute | solution.py:337
  13.7 3.0 %collective-permute-start.2 = (bf16[1168,128]{1,0:T(8,128)(2,1)S(1)}, bf16[1168,128]{1,0:T(8,128)(2,1)S(1)}, u32[]{:S(2)}, u32[]{:S(2)}) collective-permute-start(bf16[1168,128]{1,0:T(8,128)(2,1)S(1)} %get-tuple-element.20.out_ref), channel_id=1, source_target_pairs={{1,2},{3,4},{5,6},{2,1},{4,3},{6,5},{9,10},{11,12},{13,14},{10,9},... | collective-permute-start | bytes 897032 | tf_op jit(solution)/shard_map/ppermute | solution.py:337
  16.7 0.0 collective-permute-done.3.pair_ref
  16.7 4.4 %inner.1 = (f32[784,128]{1,0:T(8,128)S(1)}, f32[320,256]{1,0:T(8,128)S(1)}) custom-call(bf16[1168,128]{1,0:T(8,128)(2,1)S(1)} %get-tuple-element.20.out_ref, bf16[1168,128]{1,0:T(8,128)(2,1)S(1)} %get-tuple-element.21.in_ref, bf16[1168,128]{1,0:T(8,128)(2,1)S(1)} %collective-permute-done.3.pair_ref, ...), custom_call_target="tpu_custom_call" | custom-call | flops 3000000000 | bytes 6000000 | tf_op jit(solution)/shard_map/inner/pallas_call | solution.py:276
  21.1 0.7 %collective-permute-done.2.cross_ref = bf16[1168,128]{1,0:T(8,128)(2,1)S(1)} collective-permute-done((bf16[1168,128]{1,0:T(8,128)(2,1)S(1)}, bf16[1168,128]{1,0:T(8,128)(2,1)S(1)}, u32[]{:S(2)}, u32[]{:S(2)}) %collective-permute-start.2) | collective-permute-done | bytes 299040 | tf_op jit(solution)/shard_map/ppermute | solution.py:337
  21.8 2.1 %outer.1 = (f32[784,128]{1,0:T(8,128)}, f32[49,2,2,64]{3,2,1,0:T(2,128)}) custom-call(bf16[1168,128]{1,0:T(8,128)(2,1)S(1)} %collective-permute-done.2.cross_ref, bf16[7,3,7,128,128]{4,3,2,1,0:T(8,128)(2,1)S(1)} %get-tuple-element.19.tables_ref.tables, f32[784,128]{1,0:T(8,128)S(1)} %get-tuple-element.22.part_ref, f32[320,256]{1,0:T(8,128)S(1)} %get-tuple-element.23.sums_ref), custom_call_target="tpu_custom_call" | custom-call | flops 1000000000 | bytes 5000000 | tf_op jit(solution)/shard_map/outer/pallas_call | solution.py:314
Async XLA Ops:
  2.3 9.7 %collective-permute-start = (bf16[528,128]{1,0:T(8,128)(2,1)S(1)}, bf16[528,128]{1,0:T(8,128)(2,1)S(1)}, u32[]{:S(2)}, u32[]{:S(2)}) collective-permute-start(bf16[528,128]{1,0:T(8,128)(2,1)S(1)} %get-tuple-element.15.mine_ref), channel_id=1, source_target_pairs={{8,16},{24,32},{40,48},{56,64},{72,80},{88,96},{104,112},{120,128}... | collective-permute-start | bytes 405512 | tf_op jit(solution)/shard_map/ppermute | solution.py:337
  6.5 5.5 %collective-permute-start.1 = (bf16[528,128]{1,0:T(8,128)(2,1)S(1)}, bf16[528,128]{1,0:T(8,128)(2,1)S(1)}, u32[]{:S(2)}, u32[]{:S(2)}) collective-permute-start(bf16[528,128]{1,0:T(8,128)(2,1)S(1)} %get-tuple-element.16), channel_id=1, source_target_pairs={{0,8},{16,24},{32,40},{48,56},{64,72},{80,88},{96,104},{112,120},{... | collective-permute-start | bytes 405512 | tf_op jit(solution)/shard_map/ppermute | solution.py:337
  12.1 4.7 %collective-permute-start.3 = (bf16[1168,128]{1,0:T(8,128)(2,1)S(1)}, bf16[1168,128]{1,0:T(8,128)(2,1)S(1)}, u32[]{:S(2)}, u32[]{:S(2)}) collective-permute-start(bf16[1168,128]{1,0:T(8,128)(2,1)S(1)} %get-tuple-element.21.in_ref), channel_id=1, source_target_pairs={{0,1},{2,3},{4,5},{6,7},{1,0},{3,2},{5,4},{7,6},{8,9},{10,11},{12,... | collective-permute-start | bytes 897032 | tf_op jit(solution)/shard_map/ppermute | solution.py:337
  13.7 8.1 %collective-permute-start.2 = (bf16[1168,128]{1,0:T(8,128)(2,1)S(1)}, bf16[1168,128]{1,0:T(8,128)(2,1)S(1)}, u32[]{:S(2)}, u32[]{:S(2)}) collective-permute-start(bf16[1168,128]{1,0:T(8,128)(2,1)S(1)} %get-tuple-element.20.out_ref), channel_id=1, source_target_pairs={{1,2},{3,4},{5,6},{2,1},{4,3},{6,5},{9,10},{11,12},{13,14},{10,9},... | collective-permute-start | bytes 897032 | tf_op jit(solution)/shard_map/ppermute | solution.py:337

commit v6 on v5

--- a/solution.py
+++ b/solution.py
@@ -50,13 +50,13 @@
     get_up.start()
     pairs[...] = jnp.zeros_like(pairs)
     brick[pl.ds(16 * COEF, 16 * (SLOT - COEF)), :] = jnp.zeros((16 * (SLOT - COEF), NY), F32)
+    get_own.wait()
     get_up.wait()
     wide[...] = up[...].astype(F32)
     for child in range(8):
         block = wide[pl.ds(child, COEF, stride=8), :].astype(BF16)
         pairs[pl.ds(SLOT * (child // 2), COEF), pl.ds(SLOT * (child % 2), COEF)] = block
     pairs_t = pairs[...].T
-    get_own.wait()
     brick[pl.ds(0, 16 * COEF), :] = own[...].astype(F32)
     cells = [brick[pl.ds(cell, SLOT, stride=16), :] for cell in range(16)]
     order = [(2 * px + cx) * 4 + 2 * zp + cz for px in range(2) for zp in range(2) for cx in range(2) for cz in range(2)]

time: 24 us -> 23.9 us (level)
  no operation moved by 1% of the time
where the time goes in v6:
time: 23.9 us; the launch traced here: 23.8 us
  Pallas kernels  11.4 us (48%)
  starting transfers between devices  9.24 us (39%)
  waiting for transfers between devices  2.43 us (10%)
  between operations  0.69 us (3%)
    ppermute x4, starting transfers between devices, exchange(): return lax.ppermute(array, axis, there + [(j, i) for i, j in there])  9.24 us
    pallas_call x1, Pallas kernels, inner(): pl.pallas_call(inner_kernel, in_specs=[vmem] * 4, out_specs=[vmem] * 2, o...  4.37 us
    pallas_call x1, Pallas kernels, make_tables(): pl.pallas_call(tables_kernel, in_specs=[pl.BlockSpec(memory_space=pltpu.H...  3.3 us
    ppermute x4, waiting for transfers between devices, exchange(): return lax.ppermute(array, axis, there + [(j, i) for i, j in there])  2.43 us
    pallas_call x1, Pallas kernels, outer(): pl.pallas_call(outer_kernel, in_specs=[vmem] * 4, out_specs=[vmem, vmem],...  2.1 us
    pallas_call x1, Pallas kernels, own_part(): pl.pallas_call(own_kernel, in_specs=[hbm] * 2, out_specs=[vmem] * 4, out_...  1.59 us
  transfers between devices with their start and end apart: 4, of which 2 were waited for; matrix products, arithmetic and copies ran while one was open for 0% of the time, Pallas kernels for 32%

profile of v6, /device:TPU:131, one launch (start us, length us, event | category | flops | bytes accessed | tf_op | source)
XLA Modules:
  0.0 23.8 jit_solution(12037076660441473638)
XLA Ops:
  0.6 1.6 %own_part.1 = (bf16[528,128]{1,0:T(8,128)(2,1)S(1)}, bf16[528,128]{1,0:T(8,128)(2,1)S(1)}, bf16[832,128]{1,0:T(8,128)(2,1)S(1)}, bf16[128,128]{1,0:T(8,128)(2,1)S(1)}) custom-call(bf16[784,128]{1,0:T(8,128)(2,1)} %bitcast.5, bf16[392,49]{1,0:T(8,128)(2,1)} %bitcast.6), custom_call_target="tpu_custom_call" | custom-call | tf_op jit(solution)/shard_map/own_part/pallas_call | solution.py:88
  2.2 4.2 %collective-permute-start = (bf16[528,128]{1,0:T(8,128)(2,1)S(1)}, bf16[528,128]{1,0:T(8,128)(2,1)S(1)}, u32[]{:S(2)}, u32[]{:S(2)}) collective-permute-start(bf16[528,128]{1,0:T(8,128)(2,1)S(1)} %get-tuple-element.15.mine_ref), channel_id=1, source_target_pairs={{8,16},{24,32},{40,48},{56,64},{72,80},{88,96},{104,112},{120,128}... | collective-permute-start | bytes 405512 | tf_op jit(solution)/shard_map/ppermute | solution.py:337
  6.4 0.4 %collective-permute-start.1 = (bf16[528,128]{1,0:T(8,128)(2,1)S(1)}, bf16[528,128]{1,0:T(8,128)(2,1)S(1)}, u32[]{:S(2)}, u32[]{:S(2)}) collective-permute-start(bf16[528,128]{1,0:T(8,128)(2,1)S(1)} %get-tuple-element.16), channel_id=1, source_target_pairs={{0,8},{16,24},{32,40},{48,56},{64,72},{80,88},{96,104},{112,120},{... | collective-permute-start | bytes 405512 | tf_op jit(solution)/shard_map/ppermute | solution.py:337
  6.8 3.3 %tables.1 = (bf16[7,3,7,128,128]{4,3,2,1,0:T(8,128)(2,1)S(1)}, bf16[49,2,2,64]{3,2,1,0:T(2,128)(2,1)}) custom-call(bf16[7,7,7,49,49]{4,3,2,1,0:T(8,128)(2,1)} %far_hbm.1, bf16[128,128]{1,0:T(8,128)(2,1)S(1)} %get-tuple-element.18.coarse_ref), custom_call_target="tpu_custom_call" | custom-call | bytes 10000000 | tf_op jit(solution)/shard_map/tables/pallas_call | solution.py:149
  10.1 1.8 %collective-permute-done.b_ref = bf16[528,128]{1,0:T(8,128)(2,1)S(1)} collective-permute-done((bf16[528,128]{1,0:T(8,128)(2,1)S(1)}, bf16[528,128]{1,0:T(8,128)(2,1)S(1)}, u32[]{:S(2)}, u32[]{:S(2)}) %collective-permute-start) | collective-permute-done | bytes 135200 | tf_op jit(solution)/shard_map/ppermute | solution.py:337
  11.9 0.0 collective-permute-done.1.a_ref
  11.9 0.1 pack.1
  12.0 1.6 %collective-permute-start.3 = (bf16[1168,128]{1,0:T(8,128)(2,1)S(1)}, bf16[1168,128]{1,0:T(8,128)(2,1)S(1)}, u32[]{:S(2)}, u32[]{:S(2)}) collective-permute-start(bf16[1168,128]{1,0:T(8,128)(2,1)S(1)} %get-tuple-element.21.in_ref), channel_id=1, source_target_pairs={{0,1},{2,3},{4,5},{6,7},{1,0},{3,2},{5,4},{7,6},{8,9},{10,11},{12,... | collective-permute-start | bytes 897032 | tf_op jit(solution)/shard_map/ppermute | solution.py:337
  13.6 3.0 %collective-permute-start.2 = (bf16[1168,128]{1,0:T(8,128)(2,1)S(1)}, bf16[1168,128]{1,0:T(8,128)(2,1)S(1)}, u32[]{:S(2)}, u32[]{:S(2)}) collective-permute-start(bf16[1168,128]{1,0:T(8,128)(2,1)S(1)} %get-tuple-element.20.out_ref), channel_id=1, source_target_pairs={{1,2},{3,4},{5,6},{2,1},{4,3},{6,5},{9,10},{11,12},{13,14},{10,9},... | collective-permute-start | bytes 897032 | tf_op jit(solution)/shard_map/ppermute | solution.py:337
  16.6 0.0 collective-permute-done.3.pair_ref
  16.6 4.4 %inner.1 = (f32[784,128]{1,0:T(8,128)S(1)}, f32[320,256]{1,0:T(8,128)S(1)}) custom-call(bf16[1168,128]{1,0:T(8,128)(2,1)S(1)} %get-tuple-element.20.out_ref, bf16[1168,128]{1,0:T(8,128)(2,1)S(1)} %get-tuple-element.21.in_ref, bf16[1168,128]{1,0:T(8,128)(2,1)S(1)} %collective-permute-done.3.pair_ref, ...), custom_call_target="tpu_custom_call" | custom-call | flops 3000000000 | bytes 6000000 | tf_op jit(solution)/shard_map/inner/pallas_call | solution.py:276
  21.0 0.7 %collective-permute-done.2.cross_ref = bf16[1168,128]{1,0:T(8,128)(2,1)S(1)} collective-permute-done((bf16[1168,128]{1,0:T(8,128)(2,1)S(1)}, bf16[1168,128]{1,0:T(8,128)(2,1)S(1)}, u32[]{:S(2)}, u32[]{:S(2)}) %collective-permute-start.2) | collective-permute-done | bytes 299040 | tf_op jit(solution)/shard_map/ppermute | solution.py:337
  21.7 2.1 %outer.1 = (f32[784,128]{1,0:T(8,128)}, f32[49,2,2,64]{3,2,1,0:T(2,128)}) custom-call(bf16[1168,128]{1,0:T(8,128)(2,1)S(1)} %collective-permute-done.2.cross_ref, bf16[7,3,7,128,128]{4,3,2,1,0:T(8,128)(2,1)S(1)} %get-tuple-element.19.tables_ref.tables, f32[784,128]{1,0:T(8,128)S(1)} %get-tuple-element.22.part_ref, f32[320,256]{1,0:T(8,128)S(1)} %get-tuple-element.23.sums_ref), custom_call_target="tpu_custom_call" | custom-call | flops 1000000000 | bytes 5000000 | tf_op jit(solution)/shard_map/outer/pallas_call | solution.py:314
Async XLA Ops:
  2.2 9.7 %collective-permute-start = (bf16[528,128]{1,0:T(8,128)(2,1)S(1)}, bf16[528,128]{1,0:T(8,128)(2,1)S(1)}, u32[]{:S(2)}, u32[]{:S(2)}) collective-permute-start(bf16[528,128]{1,0:T(8,128)(2,1)S(1)} %get-tuple-element.15.mine_ref), channel_id=1, source_target_pairs={{8,16},{24,32},{40,48},{56,64},{72,80},{88,96},{104,112},{120,128}... | collective-permute-start | bytes 405512 | tf_op jit(solution)/shard_map/ppermute | solution.py:337
  6.4 5.5 %collective-permute-start.1 = (bf16[528,128]{1,0:T(8,128)(2,1)S(1)}, bf16[528,128]{1,0:T(8,128)(2,1)S(1)}, u32[]{:S(2)}, u32[]{:S(2)}) collective-permute-start(bf16[528,128]{1,0:T(8,128)(2,1)S(1)} %get-tuple-element.16), channel_id=1, source_target_pairs={{0,8},{16,24},{32,40},{48,56},{64,72},{80,88},{96,104},{112,120},{... | collective-permute-start | bytes 405512 | tf_op jit(solution)/shard_map/ppermute | solution.py:337
  12.0 4.7 %collective-permute-start.3 = (bf16[1168,128]{1,0:T(8,128)(2,1)S(1)}, bf16[1168,128]{1,0:T(8,128)(2,1)S(1)}, u32[]{:S(2)}, u32[]{:S(2)}) collective-permute-start(bf16[1168,128]{1,0:T(8,128)(2,1)S(1)} %get-tuple-element.21.in_ref), channel_id=1, source_target_pairs={{0,1},{2,3},{4,5},{6,7},{1,0},{3,2},{5,4},{7,6},{8,9},{10,11},{12,... | collective-permute-start | bytes 897032 | tf_op jit(solution)/shard_map/ppermute | solution.py:337
  13.6 8.1 %collective-permute-start.2 = (bf16[1168,128]{1,0:T(8,128)(2,1)S(1)}, bf16[1168,128]{1,0:T(8,128)(2,1)S(1)}, u32[]{:S(2)}, u32[]{:S(2)}) collective-permute-start(bf16[1168,128]{1,0:T(8,128)(2,1)S(1)} %get-tuple-element.20.out_ref), channel_id=1, source_target_pairs={{1,2},{3,4},{5,6},{2,1},{4,3},{6,5},{9,10},{11,12},{13,14},{10,9},... | collective-permute-start | bytes 897032 | tf_op jit(solution)/shard_map/ppermute | solution.py:337

commit v7 on v6

--- a/solution.py
+++ b/solution.py
@@ -114,7 +114,7 @@
     def fetch(dx):
         return pltpu.make_async_copy(far_hbm.at[dx], far.at[dx], sems.at[dx])
 
-    for dx in range(7):
+    for dx in range(2):
         fetch(dx).start()
 
     turned = coarse_ref[...].astype(F32)
@@ -126,6 +126,11 @@
 
     def at_dx(dx, carry):
         fetch(dx).wait()
+
+        @pl.when(dx < 5)
+        def _():
+            fetch(dx + 2).start()
+
         keep = jnp.where(jnp.abs(dx - 3) <= 1, 0.0, 1.0).astype(BF16)
         for dy in range(7):
             left, right = [], []

time: 23.9 us -> 25.1 us (1.050)
  the two profiles are of different devices: /device:TPU:131 before, /device:TPU:113 now
where the time goes in v7:
time: 25.1 us; the launch traced here: 24.8 us
  Pallas kernels  13.6 us (54%)
  starting transfers between devices  9.84 us (39%)
  between operations  0.7 us (3%)
  waiting for transfers between devices  0.67 us (3%)
    ppermute x4, starting transfers between devices, exchange(): return lax.ppermute(array, axis, there + [(j, i) for i, j in there])  9.84 us
    pallas_call x1, Pallas kernels, make_tables(): pl.pallas_call(tables_kernel, in_specs=[pl.BlockSpec(memory_space=pltpu.H...  5.49 us
    pallas_call x1, Pallas kernels, inner(): pl.pallas_call(inner_kernel, in_specs=[vmem] * 4, out_specs=[vmem] * 2, o...  4.37 us
    pallas_call x1, Pallas kernels, outer(): pl.pallas_call(outer_kernel, in_specs=[vmem] * 4, out_specs=[vmem, vmem],...  2.1 us
    pallas_call x1, Pallas kernels, own_part(): pl.pallas_call(own_kernel, in_specs=[hbm] * 2, out_specs=[vmem] * 4, out_...  1.59 us
    ppermute x4, waiting for transfers between devices, exchange(): return lax.ppermute(array, axis, there + [(j, i) for i, j in there])  0.67 us
  transfers between devices with their start and end apart: 4, of which 1 were waited for; matrix products, arithmetic and copies ran while one was open for 0% of the time, Pallas kernels for 40%

profile of v7, /device:TPU:113, one launch (start us, length us, event | category | flops | bytes accessed | tf_op | source)
XLA Modules:
  0.0 24.8 jit_solution(12809993713759645350)
XLA Ops:
  0.6 1.6 %own_part.1 = (bf16[528,128]{1,0:T(8,128)(2,1)S(1)}, bf16[528,128]{1,0:T(8,128)(2,1)S(1)}, bf16[832,128]{1,0:T(8,128)(2,1)S(1)}, bf16[128,128]{1,0:T(8,128)(2,1)S(1)}) custom-call(bf16[784,128]{1,0:T(8,128)(2,1)} %bitcast.5, bf16[392,49]{1,0:T(8,128)(2,1)} %bitcast.6), custom_call_target="tpu_custom_call" | custom-call | tf_op jit(solution)/shard_map/own_part/pallas_call | solution.py:88
  2.2 2.1 %collective-permute-start = (bf16[528,128]{1,0:T(8,128)(2,1)S(1)}, bf16[528,128]{1,0:T(8,128)(2,1)S(1)}, u32[]{:S(2)}, u32[]{:S(2)}) collective-permute-start(bf16[528,128]{1,0:T(8,128)(2,1)S(1)} %get-tuple-element.15.mine_ref), channel_id=1, source_target_pairs={{8,16},{24,32},{40,48},{56,64},{72,80},{88,96},{104,112},{120,128}... | collective-permute-start | bytes 405512 | tf_op jit(solution)/shard_map/ppermute | solution.py:342
  4.3 3.4 %collective-permute-start.1 = (bf16[528,128]{1,0:T(8,128)(2,1)S(1)}, bf16[528,128]{1,0:T(8,128)(2,1)S(1)}, u32[]{:S(2)}, u32[]{:S(2)}) collective-permute-start(bf16[528,128]{1,0:T(8,128)(2,1)S(1)} %get-tuple-element.16), channel_id=1, source_target_pairs={{0,8},{16,24},{32,40},{48,56},{64,72},{80,88},{96,104},{112,120},{... | collective-permute-start | bytes 405512 | tf_op jit(solution)/shard_map/ppermute | solution.py:342
  7.7 5.5 %tables.1 = (bf16[7,3,7,128,128]{4,3,2,1,0:T(8,128)(2,1)S(1)}, bf16[49,2,2,64]{3,2,1,0:T(2,128)(2,1)}) custom-call(bf16[7,7,7,49,49]{4,3,2,1,0:T(8,128)(2,1)} %far_hbm.1, bf16[128,128]{1,0:T(8,128)(2,1)S(1)} %get-tuple-element.18.coarse_ref), custom_call_target="tpu_custom_call" | custom-call | bytes 10000000 | tf_op jit(solution)/shard_map/tables/pallas_call | solution.py:154
  13.2 0.0 collective-permute-done.b_ref
  13.3 0.0 collective-permute-done.1.a_ref
  13.3 0.1 pack.1
  13.3 1.3 %collective-permute-start.3 = (bf16[1168,128]{1,0:T(8,128)(2,1)S(1)}, bf16[1168,128]{1,0:T(8,128)(2,1)S(1)}, u32[]{:S(2)}, u32[]{:S(2)}) collective-permute-start(bf16[1168,128]{1,0:T(8,128)(2,1)S(1)} %get-tuple-element.21.in_ref), channel_id=1, source_target_pairs={{0,1},{2,3},{4,5},{6,7},{1,0},{3,2},{5,4},{7,6},{8,9},{10,11},{12,... | collective-permute-start | bytes 897032 | tf_op jit(solution)/shard_map/ppermute | solution.py:342
  14.7 3.0 %collective-permute-start.2 = (bf16[1168,128]{1,0:T(8,128)(2,1)S(1)}, bf16[1168,128]{1,0:T(8,128)(2,1)S(1)}, u32[]{:S(2)}, u32[]{:S(2)}) collective-permute-start(bf16[1168,128]{1,0:T(8,128)(2,1)S(1)} %get-tuple-element.20.out_ref), channel_id=1, source_target_pairs={{1,2},{3,4},{5,6},{2,1},{4,3},{6,5},{9,10},{11,12},{13,14},{10,9},... | collective-permute-start | bytes 897032 | tf_op jit(solution)/shard_map/ppermute | solution.py:342
  17.7 0.0 collective-permute-done.3.pair_ref
  17.7 4.4 %inner.1 = (f32[784,128]{1,0:T(8,128)S(1)}, f32[320,256]{1,0:T(8,128)S(1)}) custom-call(bf16[1168,128]{1,0:T(8,128)(2,1)S(1)} %get-tuple-element.20.out_ref, bf16[1168,128]{1,0:T(8,128)(2,1)S(1)} %get-tuple-element.21.in_ref, bf16[1168,128]{1,0:T(8,128)(2,1)S(1)} %collective-permute-done.3.pair_ref, ...), custom_call_target="tpu_custom_call" | custom-call | flops 3000000000 | bytes 6000000 | tf_op jit(solution)/shard_map/inner/pallas_call | solution.py:281
  22.1 0.7 %collective-permute-done.2.cross_ref = bf16[1168,128]{1,0:T(8,128)(2,1)S(1)} collective-permute-done((bf16[1168,128]{1,0:T(8,128)(2,1)S(1)}, bf16[1168,128]{1,0:T(8,128)(2,1)S(1)}, u32[]{:S(2)}, u32[]{:S(2)}) %collective-permute-start.2) | collective-permute-done | bytes 299040 | tf_op jit(solution)/shard_map/ppermute | solution.py:342
  22.7 2.1 %outer.1 = (f32[784,128]{1,0:T(8,128)}, f32[49,2,2,64]{3,2,1,0:T(2,128)}) custom-call(bf16[1168,128]{1,0:T(8,128)(2,1)S(1)} %collective-permute-done.2.cross_ref, bf16[7,3,7,128,128]{4,3,2,1,0:T(8,128)(2,1)S(1)} %get-tuple-element.19.tables_ref.tables, f32[784,128]{1,0:T(8,128)S(1)} %get-tuple-element.22.part_ref, f32[320,256]{1,0:T(8,128)S(1)} %get-tuple-element.23.sums_ref), custom_call_target="tpu_custom_call" | custom-call | flops 1000000000 | bytes 5000000 | tf_op jit(solution)/shard_map/outer/pallas_call | solution.py:319
Async XLA Ops:
  2.2 11.0 %collective-permute-start = (bf16[528,128]{1,0:T(8,128)(2,1)S(1)}, bf16[528,128]{1,0:T(8,128)(2,1)S(1)}, u32[]{:S(2)}, u32[]{:S(2)}) collective-permute-start(bf16[528,128]{1,0:T(8,128)(2,1)S(1)} %get-tuple-element.15.mine_ref), channel_id=1, source_target_pairs={{8,16},{24,32},{40,48},{56,64},{72,80},{88,96},{104,112},{120,128}... | collective-permute-start | bytes 405512 | tf_op jit(solution)/shard_map/ppermute | solution.py:342
  4.3 8.9 %collective-permute-start.1 = (bf16[528,128]{1,0:T(8,128)(2,1)S(1)}, bf16[528,128]{1,0:T(8,128)(2,1)S(1)}, u32[]{:S(2)}, u32[]{:S(2)}) collective-permute-start(bf16[528,128]{1,0:T(8,128)(2,1)S(1)} %get-tuple-element.16), channel_id=1, source_target_pairs={{0,8},{16,24},{32,40},{48,56},{64,72},{80,88},{96,104},{112,120},{... | collective-permute-start | bytes 405512 | tf_op jit(solution)/shard_map/ppermute | solution.py:342
  13.3 4.3 %collective-permute-start.3 = (bf16[1168,128]{1,0:T(8,128)(2,1)S(1)}, bf16[1168,128]{1,0:T(8,128)(2,1)S(1)}, u32[]{:S(2)}, u32[]{:S(2)}) collective-permute-start(bf16[1168,128]{1,0:T(8,128)(2,1)S(1)} %get-tuple-element.21.in_ref), channel_id=1, source_target_pairs={{0,1},{2,3},{4,5},{6,7},{1,0},{3,2},{5,4},{7,6},{8,9},{10,11},{12,... | collective-permute-start | bytes 897032 | tf_op jit(solution)/shard_map/ppermute | solution.py:342
  14.7 8.1 %collective-permute-start.2 = (bf16[1168,128]{1,0:T(8,128)(2,1)S(1)}, bf16[1168,128]{1,0:T(8,128)(2,1)S(1)}, u32[]{:S(2)}, u32[]{:S(2)}) collective-permute-start(bf16[1168,128]{1,0:T(8,128)(2,1)S(1)} %get-tuple-element.20.out_ref), channel_id=1, source_target_pairs={{1,2},{3,4},{5,6},{2,1},{4,3},{6,5},{9,10},{11,12},{13,14},{10,9},... | collective-permute-start | bytes 897032 | tf_op jit(solution)/shard_map/ppermute | solution.py:342

commit v8 on v6

--- a/solution.py
+++ b/solution.py
@@ -67,11 +67,15 @@
     b_ref[pl.ds(0, 2 * BLOCK), :] = packed_ref[pl.ds(pl.multiple_of(odd * 2 * BLOCK, 16), 2 * BLOCK), :]
     lane = lax.broadcasted_iota(jnp.int32, (SLOT, NY), 1)
     even = 2 * lax.rem(lane, HY)
+    every = jnp.concatenate(
+        [jnp.concatenate([cells[cell] for cell in order[4 * at : 4 * at + 4]], axis=0).astype(BF16) for at in range(4)],
+        axis=1,
+    )
+    product = dot(pairs_t, every)
     for zp in range(2):
         found = []
         for px in range(2):
-            part = jnp.concatenate([cells[cell] for cell in order[8 * px + 4 * zp : 8 * px + 4 * zp + 4]], axis=0)
-            both = dot(pairs_t, part.astype(BF16))
+            both = product[:, (2 * px + zp) * NY : (2 * px + zp + 1) * NY]
             first = jnp.take_along_axis(both[0:SLOT], even, axis=1, mode="promise_in_bounds")
             second = jnp.take_along_axis(both[SLOT:128], even + 1, axis=1, mode="promise_in_bounds")
             found.append(first + second)

time: 23.9 us -> 23.9 us (level)
  no operation moved by 1% of the time
where the time goes in v8:
time: 23.9 us; the launch traced here: 23.8 us
  Pallas kernels  11.4 us (48%)
  starting transfers between devices  9.24 us (39%)
  waiting for transfers between devices  2.43 us (10%)
  between operations  0.69 us (3%)
    ppermute x4, starting transfers between devices, exchange(): return lax.ppermute(array, axis, there + [(j, i) for i, j in there])  9.24 us
    pallas_call x1, Pallas kernels, inner(): pl.pallas_call(inner_kernel, in_specs=[vmem] * 4, out_specs=[vmem] * 2, o...  4.37 us
    pallas_call x1, Pallas kernels, make_tables(): pl.pallas_call(tables_kernel, in_specs=[pl.BlockSpec(memory_space=pltpu.H...  3.3 us
    ppermute x4, waiting for transfers between devices, exchange(): return lax.ppermute(array, axis, there + [(j, i) for i, j in there])  2.43 us
    pallas_call x1, Pallas kernels, outer(): pl.pallas_call(outer_kernel, in_specs=[vmem] * 4, out_specs=[vmem, vmem],...  2.1 us
    pallas_call x1, Pallas kernels, own_part(): pl.pallas_call(own_kernel, in_specs=[hbm] * 2, out_specs=[vmem] * 4, out_...  1.61 us
  transfers between devices with their start and end apart: 4, of which 2 were waited for; matrix products, arithmetic and copies ran while one was open for 0% of the time, Pallas kernels for 32%

profile of v8, /device:TPU:131, one launch (start us, length us, event | category | flops | bytes accessed | tf_op | source)
XLA Modules:
  0.0 23.8 jit_solution(4132398747026334461)
XLA Ops:
  0.6 1.6 %own_part.1 = (bf16[528,128]{1,0:T(8,128)(2,1)S(1)}, bf16[528,128]{1,0:T(8,128)(2,1)S(1)}, bf16[832,128]{1,0:T(8,128)(2,1)S(1)}, bf16[128,128]{1,0:T(8,128)(2,1)S(1)}) custom-call(bf16[784,128]{1,0:T(8,128)(2,1)} %bitcast.5, bf16[392,49]{1,0:T(8,128)(2,1)} %bitcast.6), custom_call_target="tpu_custom_call" | custom-call | tf_op jit(solution)/shard_map/own_part/pallas_call | solution.py:92
  2.2 4.2 %collective-permute-start = (bf16[528,128]{1,0:T(8,128)(2,1)S(1)}, bf16[528,128]{1,0:T(8,128)(2,1)S(1)}, u32[]{:S(2)}, u32[]{:S(2)}) collective-permute-start(bf16[528,128]{1,0:T(8,128)(2,1)S(1)} %get-tuple-element.15.mine_ref), channel_id=1, source_target_pairs={{8,16},{24,32},{40,48},{56,64},{72,80},{88,96},{104,112},{120,128}... | collective-permute-start | bytes 405512 | tf_op jit(solution)/shard_map/ppermute | solution.py:341
  6.4 0.4 %collective-permute-start.1 = (bf16[528,128]{1,0:T(8,128)(2,1)S(1)}, bf16[528,128]{1,0:T(8,128)(2,1)S(1)}, u32[]{:S(2)}, u32[]{:S(2)}) collective-permute-start(bf16[528,128]{1,0:T(8,128)(2,1)S(1)} %get-tuple-element.16), channel_id=1, source_target_pairs={{0,8},{16,24},{32,40},{48,56},{64,72},{80,88},{96,104},{112,120},{... | collective-permute-start | bytes 405512 | tf_op jit(solution)/shard_map/ppermute | solution.py:341
  6.8 3.3 %tables.1 = (bf16[7,3,7,128,128]{4,3,2,1,0:T(8,128)(2,1)S(1)}, bf16[49,2,2,64]{3,2,1,0:T(2,128)(2,1)}) custom-call(bf16[7,7,7,49,49]{4,3,2,1,0:T(8,128)(2,1)} %far_hbm.1, bf16[128,128]{1,0:T(8,128)(2,1)S(1)} %get-tuple-element.18.coarse_ref), custom_call_target="tpu_custom_call" | custom-call | bytes 10000000 | tf_op jit(solution)/shard_map/tables/pallas_call | solution.py:153
  10.2 1.8 %collective-permute-done.b_ref = bf16[528,128]{1,0:T(8,128)(2,1)S(1)} collective-permute-done((bf16[528,128]{1,0:T(8,128)(2,1)S(1)}, bf16[528,128]{1,0:T(8,128)(2,1)S(1)}, u32[]{:S(2)}, u32[]{:S(2)}) %collective-permute-start) | collective-permute-done | bytes 135200 | tf_op jit(solution)/shard_map/ppermute | solution.py:341
  11.9 0.0 collective-permute-done.1.a_ref
  11.9 0.1 pack.1
  12.0 1.6 %collective-permute-start.3 = (bf16[1168,128]{1,0:T(8,128)(2,1)S(1)}, bf16[1168,128]{1,0:T(8,128)(2,1)S(1)}, u32[]{:S(2)}, u32[]{:S(2)}) collective-permute-start(bf16[1168,128]{1,0:T(8,128)(2,1)S(1)} %get-tuple-element.21.in_ref), channel_id=1, source_target_pairs={{0,1},{2,3},{4,5},{6,7},{1,0},{3,2},{5,4},{7,6},{8,9},{10,11},{12,... | collective-permute-start | bytes 897032 | tf_op jit(solution)/shard_map/ppermute | solution.py:341
  13.6 3.0 %collective-permute-start.2 = (bf16[1168,128]{1,0:T(8,128)(2,1)S(1)}, bf16[1168,128]{1,0:T(8,128)(2,1)S(1)}, u32[]{:S(2)}, u32[]{:S(2)}) collective-permute-start(bf16[1168,128]{1,0:T(8,128)(2,1)S(1)} %get-tuple-element.20.out_ref), channel_id=1, source_target_pairs={{1,2},{3,4},{5,6},{2,1},{4,3},{6,5},{9,10},{11,12},{13,14},{10,9},... | collective-permute-start | bytes 897032 | tf_op jit(solution)/shard_map/ppermute | solution.py:341
  16.6 0.0 collective-permute-done.3.pair_ref
  16.7 4.4 %inner.1 = (f32[784,128]{1,0:T(8,128)S(1)}, f32[320,256]{1,0:T(8,128)S(1)}) custom-call(bf16[1168,128]{1,0:T(8,128)(2,1)S(1)} %get-tuple-element.20.out_ref, bf16[1168,128]{1,0:T(8,128)(2,1)S(1)} %get-tuple-element.21.in_ref, bf16[1168,128]{1,0:T(8,128)(2,1)S(1)} %collective-permute-done.3.pair_ref, ...), custom_call_target="tpu_custom_call" | custom-call | flops 3000000000 | bytes 6000000 | tf_op jit(solution)/shard_map/inner/pallas_call | solution.py:280
  21.0 0.7 %collective-permute-done.2.cross_ref = bf16[1168,128]{1,0:T(8,128)(2,1)S(1)} collective-permute-done((bf16[1168,128]{1,0:T(8,128)(2,1)S(1)}, bf16[1168,128]{1,0:T(8,128)(2,1)S(1)}, u32[]{:S(2)}, u32[]{:S(2)}) %collective-permute-start.2) | collective-permute-done | bytes 299040 | tf_op jit(solution)/shard_map/ppermute | solution.py:341
  21.7 2.1 %outer.1 = (f32[784,128]{1,0:T(8,128)}, f32[49,2,2,64]{3,2,1,0:T(2,128)}) custom-call(bf16[1168,128]{1,0:T(8,128)(2,1)S(1)} %collective-permute-done.2.cross_ref, bf16[7,3,7,128,128]{4,3,2,1,0:T(8,128)(2,1)S(1)} %get-tuple-element.19.tables_ref.tables, f32[784,128]{1,0:T(8,128)S(1)} %get-tuple-element.22.part_ref, f32[320,256]{1,0:T(8,128)S(1)} %get-tuple-element.23.sums_ref), custom_call_target="tpu_custom_call" | custom-call | flops 1000000000 | bytes 5000000 | tf_op jit(solution)/shard_map/outer/pallas_call | solution.py:318
Async XLA Ops:
  2.2 9.7 %collective-permute-start = (bf16[528,128]{1,0:T(8,128)(2,1)S(1)}, bf16[528,128]{1,0:T(8,128)(2,1)S(1)}, u32[]{:S(2)}, u32[]{:S(2)}) collective-permute-start(bf16[528,128]{1,0:T(8,128)(2,1)S(1)} %get-tuple-element.15.mine_ref), channel_id=1, source_target_pairs={{8,16},{24,32},{40,48},{56,64},{72,80},{88,96},{104,112},{120,128}... | collective-permute-start | bytes 405512 | tf_op jit(solution)/shard_map/ppermute | solution.py:341
  6.4 5.5 %collective-permute-start.1 = (bf16[528,128]{1,0:T(8,128)(2,1)S(1)}, bf16[528,128]{1,0:T(8,128)(2,1)S(1)}, u32[]{:S(2)}, u32[]{:S(2)}) collective-permute-start(bf16[528,128]{1,0:T(8,128)(2,1)S(1)} %get-tuple-element.16), channel_id=1, source_target_pairs={{0,8},{16,24},{32,40},{48,56},{64,72},{80,88},{96,104},{112,120},{... | collective-permute-start | bytes 405512 | tf_op jit(solution)/shard_map/ppermute | solution.py:341
  12.0 4.7 %collective-permute-start.3 = (bf16[1168,128]{1,0:T(8,128)(2,1)S(1)}, bf16[1168,128]{1,0:T(8,128)(2,1)S(1)}, u32[]{:S(2)}, u32[]{:S(2)}) collective-permute-start(bf16[1168,128]{1,0:T(8,128)(2,1)S(1)} %get-tuple-element.21.in_ref), channel_id=1, source_target_pairs={{0,1},{2,3},{4,5},{6,7},{1,0},{3,2},{5,4},{7,6},{8,9},{10,11},{12,... | collective-permute-start | bytes 897032 | tf_op jit(solution)/shard_map/ppermute | solution.py:341
  13.6 8.1 %collective-permute-start.2 = (bf16[1168,128]{1,0:T(8,128)(2,1)S(1)}, bf16[1168,128]{1,0:T(8,128)(2,1)S(1)}, u32[]{:S(2)}, u32[]{:S(2)}) collective-permute-start(bf16[1168,128]{1,0:T(8,128)(2,1)S(1)} %get-tuple-element.20.out_ref), channel_id=1, source_target_pairs={{1,2},{3,4},{5,6},{2,1},{4,3},{6,5},{9,10},{11,12},{13,14},{10,9},... | collective-permute-start | bytes 897032 | tf_op jit(solution)/shard_map/ppermute | solution.py:341
